TPU v7x, 32 devices: a whole 2x2x4 slice. The times are simulated.
32 devices in a mesh: lon: 8 (over z, x), lat: 4 (over y, core).
Axes of the slice: x: 2, y: 2, z: 4, core: 2. Of those that a mesh axis runs over, the one named last changes fastest.
Arguments:
- right_side: float32 [2, 32, 64, 1024], P(None, None, 'lat', 'lon'), may hold values from -36 to 36
- sea_mask: int32 [32, 64, 1024], P(None, 'lat', 'lon'), may hold values 0 or 1
- levels: int32 [64, 1024], P('lat', 'lon'), may hold values from 0 to 32
- east_diffusivity: bfloat16 [32, 64, 1024], P(None, 'lat', 'lon'), may hold values from 1 to 8
- north_diffusivity: bfloat16 [32, 64, 1024], P(None, 'lat', 'lon'), may hold values from 1 to 8
- vertical_diffusivity: bfloat16 [32, 64, 1024], P(None, 'lat', 'lon'), may hold values from 0.5 to 8
Outputs:
- solution_field: float32 [2, 32, 64, 1024], P(None, None, 'lat', 'lon')
- residual: float32 [2, 32, 64, 1024], P(None, None, 'lat', 'lon')
All inputs are finite; a program needn't handle non-finite values. No bound on the sum of `sea_mask` on one device may be relied on, other than what follows from the above.
Results may differ from a plain program's by a relative error of at most 0.004.
Values sent between devices are 32-bit elements; how exact they have to be, the bound alone decides.
No kernel may reach another device: no remote copies, remote signals or barrier semaphores. Data moves between devices by JAX's collectives and lax.ppermute only.
A program may use at most 64 MiB of HBM per device.

v0:
```python
import jax
import jax.numpy as jnp
from jax import lax
from jax.sharding import PartitionSpec as P

ITERS = 2


def from_behind(x, axis, by):
    devices = lax.axis_size(axis)
    return lax.ppermute(x, axis, [(i, (i + by) % devices) for i in range(devices)])


def shifted(x, axis, by):
    devices = lax.axis_size(axis)
    pairs = [(i, i + by) for i in range(devices) if 0 <= i + by < devices]
    return lax.ppermute(x, axis, pairs)


def local_sum(first, second):
    return jnp.sum(first * second, axis=(1, 2, 3))


def expand(scalars):
    return scalars[:, None, None, None]


def vertical_change(field, coef_down):
    value_below = jnp.concatenate([field[:, 1:], jnp.zeros_like(field[:, :1])], axis=1)
    flux_down = coef_down * (value_below - field)
    flux_above = jnp.concatenate([jnp.zeros_like(flux_down[:, :1]), flux_down[:, :-1]], axis=1)
    return flux_above - flux_down


def body(right_side, sea_mask, levels, east_diffusivity, north_diffusivity, vertical_diffusivity):
    depth_index = lax.broadcasted_iota(jnp.int32, sea_mask.shape, 0)
    ocean_flag = ((sea_mask == 1) & (depth_index < levels[None])).astype(jnp.int32)
    east_column = from_behind(ocean_flag[:, :, :1], "lon", -1)
    north_row = shifted(ocean_flag[:, :1, :], "lat", -1)
    ocean = ocean_flag.astype(jnp.float32)
    ocean_east = jnp.concatenate([ocean[:, :, 1:], east_column.astype(jnp.float32)], axis=2)
    ocean_north = jnp.concatenate([ocean[:, 1:, :], north_row.astype(jnp.float32)], axis=1)
    ocean_below = jnp.concatenate([ocean[1:], jnp.zeros_like(ocean[:1])], axis=0)
    coef_east = east_diffusivity.astype(jnp.float32) * ocean * ocean_east
    coef_north = north_diffusivity.astype(jnp.float32) * ocean * ocean_north
    coef_down = vertical_diffusivity.astype(jnp.float32) * ocean * ocean_below
    solution = jnp.zeros_like(right_side)
    residual = right_side

    def sum_squares(field):
        return lax.psum(local_sum(field, field), ("lon", "lat"))

    direction = right_side
    norm_now = sum_squares(residual)
    for iteration in range(ITERS):
        first_column = from_behind(direction[:, :, :, :1], "lon", -1)
        first_row = shifted(direction[:, :, :1, :], "lat", -1)
        value_east = jnp.concatenate([direction[:, :, :, 1:], first_column], axis=3)
        value_north = jnp.concatenate([direction[:, :, 1:, :], first_row], axis=2)
        flux_east = coef_east * (value_east - direction)
        flux_north = coef_north * (value_north - direction)
        last_column = from_behind(flux_east[:, :, :, -1:], "lon", 1)
        last_row = shifted(flux_north[:, :, -1:, :], "lat", 1)
        flux_west = jnp.concatenate([last_column, flux_east[:, :, :, :-1]], axis=3)
        flux_south = jnp.concatenate([last_row, flux_north[:, :, :-1, :]], axis=2)
        image = (
            direction
            + (flux_west - flux_east)
            + (flux_south - flux_north)
            + vertical_change(direction, coef_down)
        )
        step_size = norm_now / lax.psum(local_sum(direction, image), ("lon", "lat"))
        solution = solution + expand(step_size) * direction
        residual = residual - expand(step_size) * image
        norm_next = sum_squares(residual)
        direction = residual + expand(norm_next / norm_now) * direction
        norm_now = norm_next
    return (solution, residual)


def solution(mesh):
    return jax.shard_map(
        body,
        mesh=mesh,
        in_specs=(
            P(None, None, "lat", "lon"),
            P(None, "lat", "lon"),
            P("lat", "lon"),
            P(None, "lat", "lon"),
            P(None, "lat", "lon"),
            P(None, "lat", "lon"),
        ),
        out_specs=(P(None, None, "lat", "lon"), P(None, None, "lat", "lon")),
        check_vma=False,
    )
```

profile of v0, /device:TPU:0, one launch (start us, length us, event | category | flops | bytes accessed | tf_op | source)
XLA Modules:
  0.0 202.0 jit_solution(5502617171312522495)
XLA Ops:
  0.6 0.0 copy-start
  0.6 1.1 fusion.14
  1.7 1.3 collective-permute-start.3
  3.0 6.0 %collective-permute-start = (s32[32,16,1]{2,1,0:T(8,128)S(1)}, s32[32,16,1]{2,1,0:T(8,128)S(1)}, u32[]{:S(2)}, u32[]{:S(2)}) collective-permute-start(s32[32,16,1]{2,1,0:T(8,128)S(1)} %bitcast.13), channel_id=1, source_target_pairs={{0,28},{4,0},{8,4},{12,8},{16,12},{20,16},{24,20},{28,24},{1,29},{... | collective-permute-start | bytes 6152 | tf_op jit(solution)/shard_map/ppermute | solution.py:11
  9.1 0.0 copy-done
  9.1 1.3 collective-permute-start.4
  10.4 0.6 collective-permute-start.1
  11.1 0.2 slice.77
  11.3 0.1 slice.100
  11.5 0.0 copy-start.1
  11.5 0.0 copy-start.2
  11.5 0.0 copy-start.3
  11.5 4.1 %collective-permute-done = s32[32,16,1]{2,1,0:T(8,128)S(1)} collective-permute-done((s32[32,16,1]{2,1,0:T(8,128)S(1)}, s32[32,16,1]{2,1,0:T(8,128)S(1)}, u32[]{:S(2)}, u32[]{:S(2)}) %collective-permute-start) | collective-permute-done | bytes 2080 | tf_op jit(solution)/shard_map/ppermute | solution.py:11
  15.6 0.0 collective-permute-done.3
  15.7 0.0 copy-done.1
  15.7 0.0 copy-done.2
  15.7 0.0 copy-done.3
  15.7 0.2 maximum_multiply_fusion
  15.9 11.0 %collective-permute-done.1 = f32[2,32,16,1]{3,2,1,0:T(8,128)S(1)} collective-permute-done((f32[2,32,16,1]{3,2,1,0:T(8,128)S(1)}, f32[2,32,16,1]{3,2,1,0:T(8,128)S(1)}, u32[]{:S(2)}, u32[]{:S(2)}) %collective-permute-start.1) | collective-permute-done | bytes 4128 | tf_op jit(solution)/shard_map/ppermute | solution.py:11
  26.8 0.0 collective-permute-done.4
  26.8 0.4 fusion
  27.2 2.3 %collective-permute-start.5 = (f32[2,32,1,128]{3,2,1,0:T(1,128)S(1)}, f32[2,32,1,128]{3,2,1,0:T(1,128)S(1)}, u32[]{:S(2)}, u32[]{:S(2)}) collective-permute-start(f32[2,32,1,128]{3,2,1,0:T(1,128)S(1)} %slice.106), channel_id=1, source_target_pairs={{0,1},{1,2},{2,3},{4,5},{5,6},{6,7},{8,9},{9,10},{10,11},{12,13},{... | collective-permute-start | bytes 98312 | tf_op jit(solution)/shard_map/ppermute | solution.py:17
  29.5 0.2 slice.102
  29.7 0.2 collective-permute-start.2
  29.9 16.4 %collective-permute-done.2 = f32[2,32,16,1]{3,2,1,0:T(8,128)S(1)} collective-permute-done((f32[2,32,16,1]{3,2,1,0:T(8,128)S(1)}, f32[2,32,16,1]{3,2,1,0:T(8,128)S(1)}, u32[]{:S(2)}, u32[]{:S(2)}) %collective-permute-start.2) | collective-permute-done | bytes 4128 | tf_op jit(solution)/shard_map/ppermute | solution.py:11
  46.3 0.0 collective-permute-done.5
  46.3 0.5 multiply_reduce_fusion.2
  46.8 36.9 %all-reduce.5 = (f32[2]{0:T(128)S(1)}, f32[2]{0:T(128)S(1)}) all-reduce(f32[2]{0:T(128)S(1)} %get-tuple-element.3, f32[2]{0:T(128)S(1)} %get-tuple-element.2), channel_id=1, replica_groups=mesh['lon'=8,'lat'=4] {'lon','lat'}, use_global_device_ids=true, to_apply=%region_1.0 | all-reduce | flops 4 | bytes 32 | tf_op jit(solution)/shard_map/psum | solution.py:51
  83.8 0.3 multiply_reduce_fusion.1
  84.0 42.0 %psum.30 = f32[2]{0:T(128)S(1)} all-reduce(f32[2]{0:T(128)S(1)} %multiply_reduce_fusion.1), channel_id=1, replica_groups=mesh['lon'=8,'lat'=4] {'lon','lat'}, use_global_device_ids=true, to_apply=%region_5.0 | all-reduce | flops 2 | bytes 16 | tf_op jit(solution)/shard_map/psum | solution.py:51
  126.1 0.1 multiply_add_fusion.1
  126.3 1.3 collective-permute-start.8
  127.6 3.4 %collective-permute-start.6 = (f32[2,32,16,1]{3,2,1,0:T(8,128)S(1)}, f32[2,32,16,1]{3,2,1,0:T(8,128)S(1)}, u32[]{:S(2)}, u32[]{:S(2)}) collective-permute-start(f32[2,32,16,1]{3,2,1,0:T(8,128)S(1)} %bitcast.8), channel_id=1, source_target_pairs={{0,28},{4,0},{8,4},{12,8},{16,12},{20,16},{24,20},{28,24},{1,29},{... | collective-permute-start | bytes 12296 | tf_op jit(solution)/shard_map/ppermute | solution.py:11
  131.1 0.2 slice.110
  131.3 11.9 %collective-permute-done.6 = f32[2,32,16,1]{3,2,1,0:T(8,128)S(1)} collective-permute-done((f32[2,32,16,1]{3,2,1,0:T(8,128)S(1)}, f32[2,32,16,1]{3,2,1,0:T(8,128)S(1)}, u32[]{:S(2)}, u32[]{:S(2)}) %collective-permute-start.6) | collective-permute-done | bytes 4128 | tf_op jit(solution)/shard_map/ppermute | solution.py:11
  143.2 0.0 collective-permute-done.8
  143.2 0.4 fusion.5
  143.6 2.3 %collective-permute-start.9 = (f32[2,32,1,128]{3,2,1,0:T(1,128)S(1)}, f32[2,32,1,128]{3,2,1,0:T(1,128)S(1)}, u32[]{:S(2)}, u32[]{:S(2)}) collective-permute-start(f32[2,32,1,128]{3,2,1,0:T(1,128)S(1)} %slice.116), channel_id=1, source_target_pairs={{0,1},{1,2},{2,3},{4,5},{5,6},{6,7},{8,9},{9,10},{10,11},{12,13},{... | collective-permute-start | bytes 98312 | tf_op jit(solution)/shard_map/ppermute | solution.py:17
  145.8 0.2 slice.112
  146.0 2.1 %collective-permute-start.7 = (f32[2,32,16,1]{3,2,1,0:T(8,128)S(1)}, f32[2,32,16,1]{3,2,1,0:T(8,128)S(1)}, u32[]{:S(2)}, u32[]{:S(2)}) collective-permute-start(f32[2,32,16,1]{3,2,1,0:T(8,128)S(1)} %slice.112), channel_id=1, source_target_pairs={{0,4},{4,8},{8,12},{12,16},{16,20},{20,24},{24,28},{28,0},{1,5},{5... | collective-permute-start | bytes 12296 | tf_op jit(solution)/shard_map/ppermute | solution.py:11
  148.1 15.4 %collective-permute-done.7 = f32[2,32,16,1]{3,2,1,0:T(8,128)S(1)} collective-permute-done((f32[2,32,16,1]{3,2,1,0:T(8,128)S(1)}, f32[2,32,16,1]{3,2,1,0:T(8,128)S(1)}, u32[]{:S(2)}, u32[]{:S(2)}) %collective-permute-start.7) | collective-permute-done | bytes 4128 | tf_op jit(solution)/shard_map/ppermute | solution.py:11
  163.5 0.0 collective-permute-done.9
  163.5 0.5 multiply_reduce_fusion
  164.0 36.8 %psum.31 = f32[2]{0:T(128)S(1)} all-reduce(f32[2]{0:T(128)S(1)} %get-tuple-element.6), channel_id=1, replica_groups=mesh['lon'=8,'lat'=4] {'lon','lat'}, use_global_device_ids=true, to_apply=%region_7.0 | all-reduce | flops 2 | bytes 16 | tf_op jit(solution)/shard_map/psum | solution.py:72
  200.8 1.2 multiply_subtract_fusion
  (18 shorter events, 0.4 us)
Async XLA Ops:
  0.6 8.4 %copy-start = (f32[2,32,16,128]{3,2,1,0:T(8,128)S(1)}, f32[2,32,16,128]{3,2,1,0:T(8,128)}, u32[]{:S(2)}) copy-start(f32[2,32,16,128]{3,2,1,0:T(8,128)} %param.6) | copy-start | bytes 1572868
  1.7 13.9 %collective-permute-start.3 = (s32[32,1,128]{2,1,0:T(1,128)S(1)}, s32[32,1,128]{2,1,0:T(1,128)S(1)}, u32[]{:S(2)}, u32[]{:S(2)}) collective-permute-start(s32[32,1,128]{2,1,0:T(1,128)S(1)} %slice.105), channel_id=1, source_target_pairs={{1,0},{2,1},{3,2},{5,4},{6,5},{7,6},{9,8},{10,9},{11,10},{13,12},{... | collective-permute-start | bytes 49160 | tf_op jit(solution)/shard_map/ppermute | solution.py:17
  3.0 12.6 %collective-permute-start = (s32[32,16,1]{2,1,0:T(8,128)S(1)}, s32[32,16,1]{2,1,0:T(8,128)S(1)}, u32[]{:S(2)}, u32[]{:S(2)}) collective-permute-start(s32[32,16,1]{2,1,0:T(8,128)S(1)} %bitcast.13), channel_id=1, source_target_pairs={{0,28},{4,0},{8,4},{12,8},{16,12},{20,16},{24,20},{28,24},{1,29},{... | collective-permute-start | bytes 6152 | tf_op jit(solution)/shard_map/ppermute | solution.py:11
  9.1 17.8 %collective-permute-start.4 = (f32[2,32,1,128]{3,2,1,0:T(1,128)S(1)}, f32[2,32,1,128]{3,2,1,0:T(1,128)S(1)}, u32[]{:S(2)}, u32[]{:S(2)}) collective-permute-start(f32[2,32,1,128]{3,2,1,0:T(1,128)S(1)} %slice.84), channel_id=1, source_target_pairs={{1,0},{2,1},{3,2},{5,4},{6,5},{7,6},{9,8},{10,9},{11,10},{13,12},{... | collective-permute-start | bytes 98312 | tf_op jit(solution)/shard_map/ppermute | solution.py:17
  10.4 16.5 %collective-permute-start.1 = (f32[2,32,16,1]{3,2,1,0:T(8,128)S(1)}, f32[2,32,16,1]{3,2,1,0:T(8,128)S(1)}, u32[]{:S(2)}, u32[]{:S(2)}) collective-permute-start(f32[2,32,16,1]{3,2,1,0:T(8,128)S(1)} %bitcast.7), channel_id=1, source_target_pairs={{0,28},{4,0},{8,4},{12,8},{16,12},{20,16},{24,20},{28,24},{1,29},{... | collective-permute-start | bytes 12296 | tf_op jit(solution)/shard_map/ppermute | solution.py:11
  11.5 4.2 %copy-start.1 = (bf16[32,16,128]{2,1,0:T(8,128)(2,1)S(1)}, bf16[32,16,128]{2,1,0:T(8,128)(2,1)}, u32[]{:S(2)}) copy-start(bf16[32,16,128]{2,1,0:T(8,128)(2,1)} %param.9) | copy-start | bytes 393220
  11.5 4.2 %copy-start.2 = (bf16[32,16,128]{2,1,0:T(8,128)(2,1)S(1)}, bf16[32,16,128]{2,1,0:T(8,128)(2,1)}, u32[]{:S(2)}) copy-start(bf16[32,16,128]{2,1,0:T(8,128)(2,1)} %param.10) | copy-start | bytes 393220
  11.5 4.2 %copy-start.3 = (bf16[32,16,128]{2,1,0:T(8,128)(2,1)S(1)}, bf16[32,16,128]{2,1,0:T(8,128)(2,1)}, u32[]{:S(2)}) copy-start(bf16[32,16,128]{2,1,0:T(8,128)(2,1)} %param.11) | copy-start | bytes 393220
  27.2 19.1 %collective-permute-start.5 = (f32[2,32,1,128]{3,2,1,0:T(1,128)S(1)}, f32[2,32,1,128]{3,2,1,0:T(1,128)S(1)}, u32[]{:S(2)}, u32[]{:S(2)}) collective-permute-start(f32[2,32,1,128]{3,2,1,0:T(1,128)S(1)} %slice.106), channel_id=1, source_target_pairs={{0,1},{1,2},{2,3},{4,5},{5,6},{6,7},{8,9},{9,10},{10,11},{12,13},{... | collective-permute-start | bytes 98312 | tf_op jit(solution)/shard_map/ppermute | solution.py:17
  29.7 16.6 %collective-permute-start.2 = (f32[2,32,16,1]{3,2,1,0:T(8,128)S(1)}, f32[2,32,16,1]{3,2,1,0:T(8,128)S(1)}, u32[]{:S(2)}, u32[]{:S(2)}) collective-permute-start(f32[2,32,16,1]{3,2,1,0:T(8,128)S(1)} %slice.102), channel_id=1, source_target_pairs={{0,4},{4,8},{8,12},{12,16},{16,20},{20,24},{24,28},{28,0},{1,5},{5... | collective-permute-start | bytes 12296 | tf_op jit(solution)/shard_map/ppermute | solution.py:11
  126.3 16.9 %collective-permute-start.8 = (f32[2,32,1,128]{3,2,1,0:T(1,128)S(1)}, f32[2,32,1,128]{3,2,1,0:T(1,128)S(1)}, u32[]{:S(2)}, u32[]{:S(2)}) collective-permute-start(f32[2,32,1,128]{3,2,1,0:T(1,128)S(1)} %slice.115), channel_id=1, source_target_pairs={{1,0},{2,1},{3,2},{5,4},{6,5},{7,6},{9,8},{10,9},{11,10},{13,12},{... | collective-permute-start | bytes 98312 | tf_op jit(solution)/shard_map/ppermute | solution.py:17
  127.6 15.6 %collective-permute-start.6 = (f32[2,32,16,1]{3,2,1,0:T(8,128)S(1)}, f32[2,32,16,1]{3,2,1,0:T(8,128)S(1)}, u32[]{:S(2)}, u32[]{:S(2)}) collective-permute-start(f32[2,32,16,1]{3,2,1,0:T(8,128)S(1)} %bitcast.8), channel_id=1, source_target_pairs={{0,28},{4,0},{8,4},{12,8},{16,12},{20,16},{24,20},{28,24},{1,29},{... | collective-permute-start | bytes 12296 | tf_op jit(solution)/shard_map/ppermute | solution.py:11
  143.6 20.0 %collective-permute-start.9 = (f32[2,32,1,128]{3,2,1,0:T(1,128)S(1)}, f32[2,32,1,128]{3,2,1,0:T(1,128)S(1)}, u32[]{:S(2)}, u32[]{:S(2)}) collective-permute-start(f32[2,32,1,128]{3,2,1,0:T(1,128)S(1)} %slice.116), channel_id=1, source_target_pairs={{0,1},{1,2},{2,3},{4,5},{5,6},{6,7},{8,9},{9,10},{10,11},{12,13},{... | collective-permute-start | bytes 98312 | tf_op jit(solution)/shard_map/ppermute | solution.py:17
  146.0 17.5 %collective-permute-start.7 = (f32[2,32,16,1]{3,2,1,0:T(8,128)S(1)}, f32[2,32,16,1]{3,2,1,0:T(8,128)S(1)}, u32[]{:S(2)}, u32[]{:S(2)}) collective-permute-start(f32[2,32,16,1]{3,2,1,0:T(8,128)S(1)} %slice.112), channel_id=1, source_target_pairs={{0,4},{4,8},{8,12},{12,16},{16,20},{20,24},{24,28},{28,0},{1,5},{5... | collective-permute-start | bytes 12296 | tf_op jit(solution)/shard_map/ppermute | solution.py:11
where the time goes:
time: 203 us; the launch traced here: 202 us
  blocking collectives  116 us (57%)
  waiting for transfers between devices  58.8 us (29%)
  starting transfers between devices  20.7 us (10%)
  other arithmetic  4.63 us (2%)
    psum x2, blocking collectives, sum_squares(): return lax.psum(local_sum(field, field), ('lon', 'lat'))  79 us
    ppermute x5, waiting for transfers between devices, from_behind(): lax.ppermute(x, axis, [(i, (i + by) % devices) for i in range(devices)])  58.8 us
    psum x1, blocking collectives, body(): step_size = norm_now / lax.psum(local_sum(direction, image), ('lon', 'lat'))  36.8 us
    ppermute x5, starting transfers between devices, from_behind(): lax.ppermute(x, axis, [(i, (i + by) % devices) for i in range(devices)])  12.3 us
    ppermute x5, starting transfers between devices, shifted(): return lax.ppermute(x, axis, pairs)  8.38 us
  transfers between devices with their start and end apart: 10, of which 5 were waited for; matrix products, arithmetic and copies ran while one was open for 1% of the time, Pallas kernels for 0%

commit v1 on v0

v1 whole, which is shorter than its diff:
```python
import functools

import jax
import jax.numpy as jnp
from jax import lax
from jax.experimental import pallas as pl
from jax.experimental.pallas import tpu as pltpu
from jax.sharding import PartitionSpec as P

F32 = jnp.float32
CHUNK = 8
SIDES = 2
FIELDS = 6


def iota(shape, axis):
    return lax.broadcasted_iota(jnp.int32, shape, axis)


def is_even(axis):
    return (lax.axis_index(axis) & 1) == 0


def levels_of(ref, first, count, rows):
    return ref[pl.ds(first * rows, count * rows), :].reshape(count, rows, ref.shape[1])


def put_levels(ref, first, value):
    count, rows, lanes = value.shape
    ref[pl.ds(first * rows, count * rows), :] = value.reshape(count * rows, lanes)


def laplacian(value, below, flux_above, east_coef, north_coef, down_coef):
    _, rows, lanes = value.shape
    flux_east = east_coef * (pltpu.roll(value, lanes - 1, 2) - value)
    flux_north = north_coef * (pltpu.roll(value, rows - 1, 1) - value)
    flux_down = down_coef * (jnp.concatenate([value[1:], below], axis=0) - value)
    from_above = jnp.concatenate([flux_above, flux_down[:-1]], axis=0)
    change = (pltpu.roll(flux_east, 1, 2) - flux_east) + (pltpu.roll(flux_north, 1, 1) - flux_north)
    return change + (from_above - flux_down), flux_down[-1:]


def packed_into(total, planes, slot, pair):
    moved = [pltpu.roll(planes[i], 2 * (slot + i) + 1, 1) for i in range(planes.shape[0])]
    for i, plane in enumerate(moved):
        total = jnp.where(pair == slot + i, plane, total)
    return total


def unpacked(packed, slot, count, offset=1):
    lanes = packed.shape[1]
    return jnp.stack([pltpu.roll(packed, (2 * lanes - offset - 2 * (slot + i)) % lanes, 1) for i in range(count)])


def spread(plane, slot, pair, level):
    moved = pltpu.roll(plane, 2 * slot + 1, 1, stride=2, stride_axis=0)
    return jnp.sum(jnp.where(pair == level + slot, moved, 0.0), axis=0, keepdims=True)


def from_neighbours(east, west, even_lane):
    return jnp.where(even_lane, pltpu.roll(east, east.shape[1] - 1, 1), pltpu.roll(west, 1, 1))


def face(own, other, even_lane):
    return jnp.where(even_lane, own * (other > 0).astype(F32), other * (own > 0).astype(F32))


def prepare_kernel(tracers, nz, rows, field_in, mask_in, levels_in, east_in, north_in, down_in,
                   field, coef_east, coef_north, coef_down, east_own, rows_a, rows_b,
                   mask, levels, east, north, down, north_own, sems):
    copies = [
        pltpu.make_async_copy(a, b, sems.at[i])
        for i, (a, b) in enumerate(((levels_in, levels), (mask_in, mask), (east_in, east), (north_in, north),
                                    (down_in, down), (field_in, field)))
    ]
    for copy in copies:
        copy.start()
    for copy in copies[:-1]:
        copy.wait()
    lanes = field.shape[1]
    shape = (CHUNK, rows, lanes)
    last_lane, last_row = iota(shape, 2) == lanes - 1, iota(shape, 1) == rows - 1
    depth = levels[...]

    level = iota((CHUNK + 1, rows, lanes), 0)
    for k in range(0, nz, CHUNK):
        count = min(CHUNK + 1, nz - k)
        wet = (levels_of(mask, k, count, rows) == 1) & (level[:count] + k < depth[None])
        wet = jnp.where(wet, 1.0, 0.0)
        if count == CHUNK:
            wet = jnp.concatenate([wet, jnp.zeros((1, rows, lanes), F32)], axis=0)
        ocean = wet[:CHUNK]
        own_east = levels_of(east, k, CHUNK, rows).astype(F32) * ocean
        own_north = levels_of(north, k, CHUNK, rows).astype(F32) * ocean
        c_east = jnp.where(last_lane, 0.0, own_east * pltpu.roll(ocean, lanes - 1, 2))
        c_north = jnp.where(last_row, 0.0, own_north * pltpu.roll(ocean, rows - 1, 1))
        c_down = levels_of(down, k, CHUNK, rows).astype(F32) * ocean * wet[1:]
        for ref, value in ((east_own, own_east), (north_own, own_north), (coef_east, c_east), (coef_north, c_north), (coef_down, c_down)):
            put_levels(ref, k, value)
    copies[-1].wait()

    def edge(side):
        first, inner, between = ((0, 1, 0), (rows - 1, rows - 2, rows - 2))[side]
        c_east = coef_east[pl.ds(first, nz, rows), :]
        c_inner = coef_north[pl.ds(between, nz, rows), :]
        c_down = coef_down[pl.ds(first, nz, rows), :]
        images, values = [], []
        for t in range(tracers):
            at = t * nz * rows
            v = field[pl.ds(first + at, nz, rows), :]
            flux_east = c_east * (pltpu.roll(v, lanes - 1, 1) - v)
            flux_down = c_down * (pltpu.roll(v, nz - 1, 0) - v)
            images.append((pltpu.roll(flux_east, 1, 1) - flux_east) + c_inner * (v - field[pl.ds(inner + at, nz, rows), :])
                          + (pltpu.roll(flux_down, 1, 0) - flux_down))
            values.append(v)
        return images + values + [east_own[pl.ds(first, nz, rows), :], north_own[pl.ds(first, nz, rows), :]]

    even = is_even("lat")
    for at, (south, north_) in enumerate(zip(edge(0), edge(1))):
        rows_a[pl.ds(at * nz, nz), :] = jnp.where(even, north_, south)
        rows_b[pl.ds(at * nz, nz), :] = jnp.where(even, south, north_)


def columns_kernel(tracers, nz, rows, field, coef_east, coef_north, coef_down, east_own, image, packed):
    lanes = field.shape[1]
    pair = iota((rows, lanes), 1) >> 1
    zero = jnp.zeros((rows, lanes), F32)
    totals = [zero, zero, zero]
    above = [jnp.zeros((1, rows, lanes), F32)] * tracers
    for k in range(0, nz, CHUNK):
        c = [levels_of(ref, k, CHUNK, rows) for ref in (coef_east, coef_north, coef_down)]
        own = levels_of(east_own, k, CHUNK, rows)
        values, changes = [], []
        for t in range(tracers):
            value = levels_of(field, t * nz + k, CHUNK, rows)
            below = levels_of(field, t * nz + k + CHUNK, 1, rows) if k + CHUNK < nz else zero[None]
            change, above[t] = laplacian(value, below, above[t], *c)
            values.append(value)
            changes.append(change)
        totals[2] = packed_into(totals[2], own, k, pair)
        for t in range(tracers):
            totals[0] = packed_into(totals[0], changes[t], t * nz + k, pair)
            totals[1] = packed_into(totals[1], values[t], t * nz + k, pair)
        for t in range(tracers):
            put_levels(image, t * nz + k, changes[t])
    packed[pl.ds(0, rows), :] = totals[0]
    packed[pl.ds(rows, rows), :] = totals[1]
    total = totals[2]
    for t in range(1, tracers):
        total = total + pltpu.roll(totals[2], 2 * nz * t, 1)
    packed[pl.ds(2 * rows, rows), :] = total


def rows_kernel(tracers, nz, rows, own_a, own_b, got_a, got_b, packed, message, flux, ring, coef):
    lanes = packed.shape[1]
    even = is_even("lat")
    pair, level = iota((nz, lanes), 1) >> 1, iota((nz, lanes), 0)
    row_change, corner_field, corner_east = [], [], []
    for side in range(SIDES):
        def part(at, a, b):
            first, second = (b, a) if side == 0 else (a, b)
            return jnp.where(even, first[pl.ds(at * nz, nz), :], second[pl.ds(at * nz, nz), :])

        own = lambda at: part(at, own_a, own_b)
        got = lambda at: part(at, got_a, got_b)
        own_east, got_east = own(2 * tracers), got(2 * tracers)
        if side == 0:
            c = got(2 * tracers + 1) * (own_east > 0).astype(F32)
        else:
            c = own(2 * tracers + 1) * (got_east > 0).astype(F32)
        coef[pl.ds(side * nz, nz), :] = c
        change = beyond = edge = jnp.zeros((1, lanes), F32)
        for t in range(tracers):
            other = got(tracers + t)
            f = c * (other - own(tracers + t))
            at = pl.ds((side * tracers + t) * nz, nz)
            flux[at, :] = f
            ring[at, :] = got(t) + f
            change = change + spread(f, nz * t, pair, level)
            beyond = beyond + spread(other, nz * t, pair, level)
            edge = edge + spread(got_east, nz * t, pair, level)
        row_change.append(change)
        corner_field.append(beyond)
        corner_east.append(edge)
    row = iota((rows, lanes), 0)
    first = packed[pl.ds(0, rows), :]
    first = first - jnp.where(row == 0, row_change[0], 0.0) - jnp.where(row == rows - 1, row_change[1], 0.0)
    message[pl.ds(0, rows), :] = first
    message[pl.ds(rows, 2 * rows), :] = packed[pl.ds(rows, 2 * rows), :]
    message[pl.ds(3 * rows, 8), :] = stacked(corner_field + corner_east)


def stacked(parts):
    lanes = parts[0].shape[1]
    row = iota((8, lanes), 0)
    total = jnp.zeros((8, lanes), F32)
    for i, part in enumerate(parts):
        total = jnp.where(row == i, part, total)
    return total


def folded(x):
    return sum(x[i : i + 8] for i in range(0, x.shape[0], 8))


def interior_kernel(tracers, nz, rows, field, start, coef_east, coef_north, coef_down, flux, ring, coef,
                    image, twice, packed, beyond, sums):
    lanes = field.shape[1]
    lane = iota((rows, lanes), 1)
    pair, last_lane = lane >> 1, iota((CHUNK, rows, lanes), 2) == lanes - 1
    wide_pair, level = iota((nz, lanes), 1) >> 1, iota((nz, lanes), 0)

    image[...] = start[...]
    ring_rows, coef_rows = [], []
    for side in range(SIDES):
        c = coef[pl.ds(side * nz, nz), :]
        at_ring = at_coef = jnp.zeros((1, lanes), F32)
        for t in range(tracers):
            at = pl.ds((rows - 1) * side + t * nz * rows, nz, rows)
            part = pl.ds((side * tracers + t) * nz, nz)
            image[at, :] = start[at, :] - flux[part, :]
            at_ring = at_ring + spread(ring[part, :], nz * t, wide_pair, level)
            at_coef = at_coef + spread(c, nz * t, wide_pair, level)
        ring_rows.append(at_ring)
        coef_rows.append(at_coef)
    beyond[...] = stacked(coef_rows + ring_rows)

    zero = jnp.zeros((rows, lanes), F32)
    packed_twice, packed_north, packed_down, packed_inner = [zero] * 4
    totals = [[zero] * 4 for _ in range(tracers)]
    above = [zero[None]] * tracers
    for k in range(0, nz, CHUNK):
        c = [levels_of(ref, k, CHUNK, rows) for ref in (coef_east, coef_north, coef_down)]
        results = []
        for t in range(tracers):
            w = levels_of(image, t * nz + k, CHUNK, rows)
            below = levels_of(image, t * nz + k + CHUNK, 1, rows) if k + CHUNK < nz else zero[None]
            y, above[t] = laplacian(w, below, above[t], *c)
            results.append(y)
            v = levels_of(field, t * nz + k, CHUNK, rows)
            for i, product in enumerate((v * v, v * w, w * w, w * y)):
                totals[t][i] = totals[t][i] + jnp.sum(product, axis=0)
        inner = jnp.where(last_lane, pltpu.roll(c[0], 1, 2), c[0])
        packed_north = packed_into(packed_north, c[1], k, pair)
        packed_down = packed_into(packed_down, c[2], k, pair)
        packed_inner = packed_into(packed_inner, inner, k, pair)
        for t in range(tracers):
            packed_twice = packed_into(packed_twice, results[t], t * nz + k, pair)
        for t in range(tracers):
            put_levels(twice, t * nz + k, results[t])
    packed[pl.ds(0, rows), :] = packed_twice
    for i, part in enumerate((packed_north, packed_down, packed_inner)):
        whole = part
        for t in range(1, tracers):
            whole = whole + pltpu.roll(part, 2 * nz * t, 1)
        packed[pl.ds((i + 1) * rows, rows), :] = whole
    for t in range(tracers):
        last = jnp.zeros((nz, lanes), F32)
        for side in range(SIDES):
            at = pl.ds((rows - 1) * side + t * nz * rows, nz, rows)
            w = image[at, :]
            change = coef[pl.ds(side * nz, nz), :] * (ring[pl.ds((side * tracers + t) * nz, nz), :] - w)
            twice[at, :] = twice[at, :] - change
            last = last - w * change
        for i in range(4):
            total = folded(totals[t][i])
            if i == 3:
                total = total + folded(last)
            sums[pl.ds((4 * t + i) * 8, 8), :] = total


def sums_kernel(tracers, nz, rows, devices, own, got_a, got_b, packed, beyond, sums, corrections, result):
    lanes = own.shape[1]
    even = is_even("lon")
    lane, row = iota((rows, lanes), 1), iota((rows, lanes), 0)
    even_lane = (lane & 1) == 0
    parts = [pl.ds(i * rows, rows) for i in range(4)]

    def neighbours(at, even_lane):
        a, b = got_a[at, :], got_b[at, :]
        return from_neighbours(jnp.where(even, a, b), jnp.where(even, b, a), even_lane)

    own_image, own_field, own_east = [own[p, :] for p in parts[:3]]
    got_image, got_field, got_east = [neighbours(p, even_lane) for p in parts[:3]]
    twice, north, down, inner = [packed[p, :] for p in parts]
    c = face(own_east, got_east, even_lane)
    f = c * (got_field - own_field)
    e = -f
    image = own_image + e
    f_twice = c * ((got_image + f) - image)
    at = pl.ds(3 * rows, 8)
    even_tile = (iota((8, lanes), 1) & 1) == 0
    own_corner, got_corner = own[at, :], neighbours(at, even_tile)
    c_corner = face(own_corner, got_corner, even_tile)
    difference = got_corner - own_corner
    lat = beyond[...]
    new_change = old_change = jnp.zeros((rows, lanes), F32)
    for side in range(SIDES):
        ring = lat[2 + side : 3 + side]
        ring_new = ring - c_corner[2 + side : 3 + side] * difference[side : side + 1]
        coef = lat[side : side + 1]
        here = row == (rows - 1) * side
        new_change = jnp.where(here, coef * (ring_new - image), new_change)
        old_change = jnp.where(here, coef * (ring - own_image), old_change)
    flux_down = down * (pltpu.roll(e, lanes - 2, 1) - e)
    flux_north = north * (pltpu.roll(e, rows - 1, 0) - e)
    inside = (pltpu.roll(flux_down, 2, 1) - flux_down) + (pltpu.roll(flux_north, 1, 0) - flux_north) + inner * e
    change = inside - f_twice - (new_change - old_change)
    beside = -inner * e
    corrections[parts[0], :] = e
    corrections[parts[1], :] = change
    corrections[parts[2], :] = jnp.where(even_lane, beside, pltpu.roll(beside, 2, 1))

    bw = folded(own_field * e)
    ww = folded((own_image + image) * e)
    wy = folded((2.0 * twice + inside) * e - image * f_twice - image * new_change + own_image * old_change)
    tile_lane, tile_row = iota((8, lanes), 1), iota((8, lanes), 0)
    total = jnp.zeros((8, lanes), F32)
    for t in range(tracers):
        mine = (tile_lane >= 2 * nz * t) & (tile_lane < 2 * nz * (t + 1))
        for i, more in enumerate((None, bw, ww, wy)):
            part = sums[pl.ds((4 * t + i) * 8, 8), :]
            if more is not None:
                part = part + jnp.where(mine, more, 0.0)
            total = jnp.where(tile_row == 4 * t + i, jnp.sum(part, axis=0, keepdims=True), total)
    total = jnp.sum(total, axis=1, keepdims=True)
    total = jnp.sum(jnp.where(tile_row == tile_lane, total, 0.0), axis=0, keepdims=True)
    result[...] = jnp.broadcast_to(total, (devices, lanes))


def finish_kernel(tracers, nz, rows, field, image, twice, corrections, sums, solution, residual):
    lanes = field.shape[1]
    total = jnp.sum(sums[...], axis=0, keepdims=True)
    one = iota((1, lanes), 1)
    lane = iota((CHUNK, rows, lanes), 2)
    edge = (lane == 0) | (lane == lanes - 1)
    inner = (lane == 1) | (lane == lanes - 2)
    e, change, beside = [corrections[pl.ds(i * rows, rows), :] for i in range(3)]

    def number(i):
        return jnp.sum(jnp.where(one == i, total, 0.0), axis=1, keepdims=True)

    for t in range(tracers):
        bb, bw, ww, wy = [number(4 * t + i) for i in range(4)]
        whole = bb + bw
        step = bb / whole
        rest = bw / whole
        new = rest * rest * bb - 2.0 * rest * step * bw + step * step * ww
        beta = new / bb
        tau = beta + rest
        step_next = new / (new + beta * beta * bb + tau * tau * bw - 2.0 * tau * step * ww + step * step * wy)
        both = step * step_next
        s_b = step + step_next * tau
        r_b = rest - step_next * tau
        r_w = both - step - step_next * tau
        s_edge = -both * e
        r_edge = r_w * e + both * change
        r_inner = both * beside
        for slot in range(t * nz, (t + 1) * nz, CHUNK):
            v, w, y = [levels_of(ref, slot, CHUNK, rows) for ref in (field, image, twice)]
            more = jnp.where(edge, unpacked(s_edge, slot, CHUNK), 0.0)
            much = jnp.where(inner, unpacked(r_inner, slot, CHUNK, 2), 0.0)
            much = jnp.where(edge, unpacked(r_edge, slot, CHUNK), much)
            put_levels(solution, slot, (s_b * v - both * w) + more)
            put_levels(residual, slot, (r_b * v + r_w * w + both * y) + much)


def swaps(devices, second, periodic):
    pairs = []
    for i in range(devices):
        j = i + 1 if (i % 2 == 0) != second else i - 1
        if periodic or 0 <= j < devices:
            pairs.append((i, j % devices))
    return pairs


def swapped(x, axis, second, periodic):
    return lax.ppermute(x, axis, swaps(lax.axis_size(axis), second, periodic))


def body(right_side, sea_mask, levels, east_diffusivity, north_diffusivity, vertical_diffusivity):
    tracers, nz, rows, lanes = right_side.shape
    devices = lax.axis_size("lon") * lax.axis_size("lat")
    flat = lambda x: x.reshape(-1, lanes)
    outside = lambda x: pltpu.with_memory_space_constraint(flat(x), pltpu.HBM)
    n = nz * rows

    def call(kernel, outs, flops, space=pltpu.VMEM, **more):
        cost = pl.CostEstimate(flops=flops, bytes_accessed=4 * lanes * sum(outs), transcendentals=0)
        return pl.pallas_call(
            functools.partial(kernel, tracers, nz, rows),
            out_shape=[space((m, lanes), F32) for m in outs],
            compiler_params=pltpu.CompilerParams(vmem_limit_bytes=32 * 1024 * 1024),
            cost_estimate=cost,
            **more,
        )

    def kernel_for(kernel):
        return lambda tracers, nz, rows, *refs: kernel(tracers, nz, rows, devices, *refs)

    cells = tracers * n * lanes
    scratch = lambda m, dtype: pltpu.VMEM((m, lanes), dtype)
    field, coef_east, coef_north, coef_down, east_own, rows_a, rows_b = call(
        prepare_kernel,
        [tracers * n, n, n, n, n, FIELDS * nz, FIELDS * nz],
        20 * cells,
        in_specs=[pl.BlockSpec(memory_space=pltpu.HBM)] * 6,
        scratch_shapes=[scratch(n, jnp.int32), scratch(rows, jnp.int32)] + [scratch(n, jnp.bfloat16)] * 3
        + [scratch(n, F32), pltpu.SemaphoreType.DMA((6,))],
        name="prepare",
    )(*map(outside, (right_side, sea_mask, levels, east_diffusivity, north_diffusivity, vertical_diffusivity)))
    got_a = swapped(rows_a, "lat", False, False)
    got_b = swapped(rows_b, "lat", True, False)
    start, packed = call(columns_kernel, [tracers * n, 3 * rows], 40 * cells, name="columns")(
        field, coef_east, coef_north, coef_down, east_own)
    edges = SIDES * tracers * nz
    message, flux, ring, coef = call(
        rows_kernel, [3 * rows + 8, edges, edges, SIDES * nz], cells, name="rows"
    )(rows_a, rows_b, got_a, got_b, packed)
    got_a = swapped(message, "lon", False, True)
    got_b = swapped(message, "lon", True, True)
    image, twice, packed, beyond, sums = call(
        interior_kernel, [tracers * n, tracers * n, 4 * rows, 8, 8 * 4 * tracers], 60 * cells, name="interior"
    )(field, start, coef_east, coef_north, coef_down, flux, ring, coef)
    corrections, sums = call(kernel_for(sums_kernel), [3 * rows, devices], cells, name="sums")(
        message, got_a, got_b, packed, beyond, sums)
    sums = lax.all_to_all(sums, ("lon", "lat"), 0, 0, tiled=True)
    solution_field, residual = call(finish_kernel, [tracers * n] * 2, 20 * cells, space=jax.ShapeDtypeStruct, name="finish")(
        field, image, twice, corrections, sums)
    return solution_field.reshape(right_side.shape), residual.reshape(right_side.shape)


def solution(mesh):
    return jax.shard_map(
        body,
        mesh=mesh,
        in_specs=(
            P(None, None, "lat", "lon"),
            P(None, "lat", "lon"),
            P("lat", "lon"),
            P(None, "lat", "lon"),
            P(None, "lat", "lon"),
            P(None, "lat", "lon"),
        ),
        out_specs=(P(None, None, "lat", "lon"), P(None, None, "lat", "lon")),
        check_vma=False,
    )
```

time: 203 us -> 31.5 us (0.16)
  blocking collectives: 116 us -> 15.2 us
  waiting for transfers between devices: 58.8 us -> 2.47 us
  starting transfers between devices: 20.7 us -> 6.79 us
  Pallas kernels: 0 us -> 6.13 us
  other arithmetic: 4.63 us -> 0 us
    psum x3 -> x0, blocking collectives: 116 us -> none  [the longest x2 79 us: sum_squares(): return lax.psum(local_sum(field, field), ('lon', 'lat'))]
    ppermute x10 -> x4, waiting for transfers between devices: 58.8 us -> 2.47 us  [swapped(): return lax.ppermute(x, axis, swaps(lax.axis_size(axis), second, periodic))]
    all_to_all x0 -> x1, blocking collectives: none -> 15.2 us  [body(): sums = lax.all_to_all(sums, ('lon', 'lat'), 0, 0, tiled=True)]
    ppermute x10 -> x4, starting transfers between devices: 20.7 us -> 6.79 us  [swapped(): return lax.ppermute(x, axis, swaps(lax.axis_size(axis), second, periodic))]
    pallas_call x0 -> x6, Pallas kernels: none -> 6.13 us  [the longest x1 1.67 us: body(): call(finish_kernel, [tracers * n] * 2, 20 * cells, space=jax.ShapeDtypeSt...]
  transfers between devices with their start and end apart: 10 -> 4, of which waited for: 5 -> 2; matrix products, arithmetic and copies ran while one was open for 1% -> 0% of each run, Pallas kernels for 0% -> 8%
where the time goes in v1:
time: 31.5 us; the launch traced here: 31.2 us
  blocking collectives  15.2 us (48%)
  starting transfers between devices  6.79 us (22%)
  Pallas kernels  6.13 us (19%)
  waiting for transfers between devices  2.47 us (8%)
  between operations  0.68 us (2%)
    all_to_all x1, blocking collectives, body(): sums = lax.all_to_all(sums, ('lon', 'lat'), 0, 0, tiled=True)  15.2 us
    ppermute x4, starting transfers between devices, swapped(): return lax.ppermute(x, axis, swaps(lax.axis_size(axis), second, periodic))  6.79 us
    ppermute x4, waiting for transfers between devices, swapped(): return lax.ppermute(x, axis, swaps(lax.axis_size(axis), second, periodic))  2.47 us
    pallas_call x1, Pallas kernels, body(): call(finish_kernel, [tracers * n] * 2, 20 * cells, space=jax.ShapeDtypeSt...  1.67 us
    pallas_call x1, Pallas kernels, body(): call(prepare_kernel, [tracers * n, n, n, n, n, FIELDS * nz, FIELDS * nz],...  1.55 us
    pallas_call x1, Pallas kernels, body(): call(interior_kernel, [tracers * n, tracers * n, 4 * rows, 8, 8 * 4 * tra...  1.4 us
    pallas_call x1, Pallas kernels, body(): call(columns_kernel, [tracers * n, 3 * rows], 40 * cells, name='columns')  1.05 us
  transfers between devices with their start and end apart: 4, of which 2 were waited for; matrix products, arithmetic and copies ran while one was open for 0% of the time, Pallas kernels for 8%

profile of v1, /device:TPU:0, one launch (start us, length us, event | category | flops | bytes accessed | tf_op | source)
XLA Modules:
  0.0 31.2 jit_solution(17427472467594436450)
XLA Ops:
  0.6 1.5 %prepare.1 = (f32[1024,128]{1,0:T(8,128)S(1)}, f32[512,128]{1,0:T(8,128)S(1)}, f32[512,128]{1,0:T(8,128)S(1)}, f32[512,128]{1,0:T(8,128)S(1)}, f32[512,128]{1,0:...) custom-call(f32[1024,128]{1,0:T(8,128)} %bitcast.13, s32[512,128]{1,0:T(8,128)} %bitcast.14, ...), custom_call_target="tpu_custom_call" | custom-call | flops 2621440 | bytes 1769472 | tf_op jit(solution)/shard_map/prepare/pallas_call | solution.py:403
  2.2 0.5 %collective-permute-start = (f32[192,128]{1,0:T(8,128)S(1)}, f32[192,128]{1,0:T(8,128)S(1)}, u32[]{:S(2)}, u32[]{:S(2)}) collective-permute-start(f32[192,128]{1,0:T(8,128)S(1)} %get-tuple-element.30.own_a), channel_id=1, source_target_pairs={{0,1},{1,0},{2,3},{3,2},{4,5},{5,4},{6,7},{7,6},{8,9},{9,8},{10,11... | collective-permute-start | bytes 294920 | tf_op jit(solution)/shard_map/ppermute | solution.py:378
  2.7 0.7 %collective-permute-start.1 = (f32[192,128]{1,0:T(8,128)S(1)}, f32[192,128]{1,0:T(8,128)S(1)}, u32[]{:S(2)}, u32[]{:S(2)}) collective-permute-start(f32[192,128]{1,0:T(8,128)S(1)} %get-tuple-element.31.own_b), channel_id=1, source_target_pairs={{1,2},{2,1},{5,6},{6,5},{9,10},{10,9},{13,14},{14,13},{17,18},{18,... | collective-permute-start | bytes 294920 | tf_op jit(solution)/shard_map/ppermute | solution.py:378
  3.4 1.1 %columns.1 = (f32[1024,128]{1,0:T(8,128)S(1)}, f32[48,128]{1,0:T(8,128)S(1)}) custom-call(f32[1024,128]{1,0:T(8,128)S(1)} %get-tuple-element.24.field, f32[512,128]{1,0:T(8,128)S(1)} %get-tuple-element.25.coef_east, f32[512,128]{1,0:T(8,128)S(1)} %get-tuple-element.26.coef_north, f32[512,128]{1,0:T(8,128)S(1)} %get-tuple-element.27.coef_down, ...), custom_call_target="tpu_custom_call" | custom-call | flops 5242880 | bytes 548864 | tf_op jit(solution)/shard_map/columns/pallas_call | solution.py:414
  4.4 0.0 collective-permute-done.got_a
  4.4 0.0 collective-permute-done.1.got_b
  4.4 0.1 rows.1
  4.6 5.6 %collective-permute-start.3 = (f32[56,128]{1,0:T(8,128)S(1)}, f32[56,128]{1,0:T(8,128)S(1)}, u32[]{:S(2)}, u32[]{:S(2)}) collective-permute-start(f32[56,128]{1,0:T(8,128)S(1)} %get-tuple-element.38.refs_0_), channel_id=1, source_target_pairs={{0,28},{4,8},{8,4},{12,16},{16,12},{20,24},{24,20},{28,0},{1,29},{... | collective-permute-start | bytes 86024 | tf_op jit(solution)/shard_map/ppermute | solution.py:378
  10.2 0.0 collective-permute-start.2
  10.2 1.4 %interior.1 = (f32[1024,128]{1,0:T(8,128)S(1)}, f32[1024,128]{1,0:T(8,128)S(1)}, f32[64,128]{1,0:T(8,128)S(1)}, f32[8,128]{1,0:T(8,128)S(1)}, f32[64,128]{1,0:T(8,128)S(1)}) custom-call(f32[1024,128]{1,0:T(8,128)S(1)} %get-tuple-element.24.field, f32[1024,128]{1,0:T(8,128)S(1)} %get-tuple-element.29.start, f32[512,128]{1,0:T(8,128)S(1)} %get-tuple-element.25.coef_east, ...), custom_call_target="tpu_custom_call" | custom-call | flops 7864320 | bytes 1118208 | tf_op jit(solution)/shard_map/interior/pallas_call | solution.py:422
  11.6 0.4 %collective-permute-done.3.refs_2_ = f32[56,128]{1,0:T(8,128)S(1)} collective-permute-done((f32[56,128]{1,0:T(8,128)S(1)}, f32[56,128]{1,0:T(8,128)S(1)}, u32[]{:S(2)}, u32[]{:S(2)}) %collective-permute-start.3) | collective-permute-done | bytes 28704 | tf_op jit(solution)/shard_map/ppermute | solution.py:378
  12.1 2.0 %collective-permute-done.2.refs_1_ = f32[56,128]{1,0:T(8,128)S(1)} collective-permute-done((f32[56,128]{1,0:T(8,128)S(1)}, f32[56,128]{1,0:T(8,128)S(1)}, u32[]{:S(2)}, u32[]{:S(2)}) %collective-permute-start.2) | collective-permute-done | bytes 28704 | tf_op jit(solution)/shard_map/ppermute | solution.py:378
  14.1 0.3 %sums.1 = (f32[48,128]{1,0:T(8,128)S(1)}, f32[32,128]{1,0:T(8,128)S(1)}) custom-call(f32[56,128]{1,0:T(8,128)S(1)} %get-tuple-element.38.refs_0_, f32[56,128]{1,0:T(8,128)S(1)} %collective-permute-done.2.refs_1_, f32[56,128]{1,0:T(8,128)S(1)} %collective-permute-done.3.refs_2_, f32[64,128]{1,0:T(8,128)S(1)} %get-tuple-element.39.refs_3_, ...), custom_call_target="tpu_custom_call" | custom-call | flops 131072 | bytes 40960 | tf_op jit(solution)/shard_map/sums/pallas_call | solution.py:425
  14.4 15.2 %all_to_all.11 = f32[32,1,128]{2,1,0:T(1,128)S(1)} all-to-all(f32[32,1,128]{2,1,0:T(1,128)S(1)} %bitcast.12), channel_id=1, replica_groups=mesh['lon'=8,'lat'=4] {'lon','lat'}, dimensions={0} | all-to-all | bytes 32768 | tf_op jit(solution)/shard_map/all_to_all | solution.py:427
  29.6 1.7 %finish.1 = (f32[1024,128]{1,0:T(8,128)}, f32[1024,128]{1,0:T(8,128)}) custom-call(f32[1024,128]{1,0:T(8,128)S(1)} %get-tuple-element.24.field, f32[1024,128]{1,0:T(8,128)S(1)} %get-tuple-element.36.image, f32[1024,128]{1,0:T(8,128)S(1)} %get-tuple-element.37.twice, f32[48,128]{1,0:T(8,128)S(1)} %get-tuple-element.42.corrections, f32[32,128]{1,0:T(8,128)S(1)} %bitcast.11), custom_call_target="tpu_custom_call" | custom-call | flops 2621440 | bytes 1048576 | tf_op jit(solution)/shard_map/finish/pallas_call | solution.py:428
Async XLA Ops:
  2.2 2.2 %collective-permute-start = (f32[192,128]{1,0:T(8,128)S(1)}, f32[192,128]{1,0:T(8,128)S(1)}, u32[]{:S(2)}, u32[]{:S(2)}) collective-permute-start(f32[192,128]{1,0:T(8,128)S(1)} %get-tuple-element.30.own_a), channel_id=1, source_target_pairs={{0,1},{1,0},{2,3},{3,2},{4,5},{5,4},{6,7},{7,6},{8,9},{9,8},{10,11... | collective-permute-start | bytes 294920 | tf_op jit(solution)/shard_map/ppermute | solution.py:378
  2.7 1.7 %collective-permute-start.1 = (f32[192,128]{1,0:T(8,128)S(1)}, f32[192,128]{1,0:T(8,128)S(1)}, u32[]{:S(2)}, u32[]{:S(2)}) collective-permute-start(f32[192,128]{1,0:T(8,128)S(1)} %get-tuple-element.31.own_b), channel_id=1, source_target_pairs={{1,2},{2,1},{5,6},{6,5},{9,10},{10,9},{13,14},{14,13},{17,18},{18,... | collective-permute-start | bytes 294920 | tf_op jit(solution)/shard_map/ppermute | solution.py:378
  4.6 7.5 %collective-permute-start.3 = (f32[56,128]{1,0:T(8,128)S(1)}, f32[56,128]{1,0:T(8,128)S(1)}, u32[]{:S(2)}, u32[]{:S(2)}) collective-permute-start(f32[56,128]{1,0:T(8,128)S(1)} %get-tuple-element.38.refs_0_), channel_id=1, source_target_pairs={{0,28},{4,8},{8,4},{12,16},{16,12},{20,24},{24,20},{28,0},{1,29},{... | collective-permute-start | bytes 86024 | tf_op jit(solution)/shard_map/ppermute | solution.py:378
  10.2 3.9 %collective-permute-start.2 = (f32[56,128]{1,0:T(8,128)S(1)}, f32[56,128]{1,0:T(8,128)S(1)}, u32[]{:S(2)}, u32[]{:S(2)}) collective-permute-start(f32[56,128]{1,0:T(8,128)S(1)} %get-tuple-element.38.refs_0_), channel_id=1, source_target_pairs={{0,4},{4,0},{8,12},{12,8},{16,20},{20,16},{24,28},{28,24},{1,5},{5... | collective-permute-start | bytes 86024 | tf_op jit(solution)/shard_map/ppermute | solution.py:378

commit v2 on v1

v2 whole, which is shorter than its diff:
```python
import functools

import jax
import jax.numpy as jnp
from jax import lax
from jax.experimental import pallas as pl
from jax.experimental.pallas import tpu as pltpu
from jax.sharding import PartitionSpec as P

F32 = jnp.float32
CHUNK = 8
SIDES = 2
FIELDS = 5


def iota(shape, axis):
    return lax.broadcasted_iota(jnp.int32, shape, axis)


def is_even(axis):
    return (lax.axis_index(axis) & 1) == 0


def levels_of(ref, first, count, rows):
    return ref[pl.ds(first * rows, count * rows), :].reshape(count, rows, ref.shape[1])


def put_levels(ref, first, value):
    count, rows, lanes = value.shape
    ref[pl.ds(first * rows, count * rows), :] = value.reshape(count * rows, lanes)


def laplacian(value, below, flux_above, east_coef, north_coef, down_coef):
    _, rows, lanes = value.shape
    flux_east = east_coef * (pltpu.roll(value, lanes - 1, 2) - value)
    flux_north = north_coef * (pltpu.roll(value, rows - 1, 1) - value)
    flux_down = down_coef * (jnp.concatenate([value[1:], below], axis=0) - value)
    from_above = jnp.concatenate([flux_above, flux_down[:-1]], axis=0)
    change = (pltpu.roll(flux_east, 1, 2) - flux_east) + (pltpu.roll(flux_north, 1, 1) - flux_north)
    return change + (from_above - flux_down), flux_down[-1:]


def packed_into(total, planes, slot, pair):
    moved = [pltpu.roll(planes[i], 2 * (slot + i) + 1, 1) for i in range(planes.shape[0])]
    for i, plane in enumerate(moved):
        total = jnp.where(pair == slot + i, plane, total)
    return total


def unpacked(packed, slot, count, offset=1):
    lanes = packed.shape[1]
    return jnp.stack([pltpu.roll(packed, (2 * lanes - offset - 2 * (slot + i)) % lanes, 1) for i in range(count)])


def spread(plane, slot, pair, level):
    moved = pltpu.roll(plane, 2 * slot + 1, 1, stride=2, stride_axis=0)
    return jnp.sum(jnp.where(pair == level + slot, moved, 0.0), axis=0, keepdims=True)


def from_neighbours(east, west, even_lane):
    return jnp.where(even_lane, pltpu.roll(east, east.shape[1] - 1, 1), pltpu.roll(west, 1, 1))


def face(own, other, even_lane):
    return jnp.where(even_lane, own * (other > 0).astype(F32), other * (own > 0).astype(F32))


def prepare_kernel(tracers, nz, rows, field_in, mask_in, levels_in, east_in, north_in, down_in,
                   field, coef_east, coef_north, coef_down, image, message, rows_a, rows_b,
                   mask, levels, east, north, down, east_own, north_own, sems):
    copies = [
        pltpu.make_async_copy(a, b, sems.at[i])
        for i, (a, b) in enumerate(((levels_in, levels), (mask_in, mask), (east_in, east), (north_in, north),
                                    (down_in, down), (field_in, field)))
    ]
    for copy in copies:
        copy.start()
    for copy in copies[:-1]:
        copy.wait()
    lanes = field.shape[1]
    shape = (CHUNK, rows, lanes)
    last_lane, last_row = iota(shape, 2) == lanes - 1, iota(shape, 1) == rows - 1
    pair = iota((rows, lanes), 1) >> 1
    zero = jnp.zeros((rows, lanes), F32)
    packed_image, packed_field, packed_east = zero, zero, zero
    depth = levels[...]
    level = iota((CHUNK + 1, rows, lanes), 0)
    for k in range(0, nz, CHUNK):
        count = min(CHUNK + 1, nz - k)
        wet = (levels_of(mask, k, count, rows) == 1) & (level[:count] + k < depth[None])
        wet = jnp.where(wet, 1.0, 0.0)
        if count == CHUNK:
            wet = jnp.concatenate([wet, zero[None]], axis=0)
        ocean = wet[:CHUNK]
        own_east = levels_of(east, k, CHUNK, rows).astype(F32) * ocean
        own_north = levels_of(north, k, CHUNK, rows).astype(F32) * ocean
        c_east = jnp.where(last_lane, 0.0, own_east * pltpu.roll(ocean, lanes - 1, 2))
        c_north = jnp.where(last_row, 0.0, own_north * pltpu.roll(ocean, rows - 1, 1))
        c_down = levels_of(down, k, CHUNK, rows).astype(F32) * ocean * wet[1:]
        packed_east = packed_into(packed_east, own_east, k, pair)
        for ref, value in ((east_own, own_east), (north_own, own_north), (coef_east, c_east), (coef_north, c_north),
                           (coef_down, c_down)):
            put_levels(ref, k, value)
    copies[-1].wait()
    above = [zero[None]] * tracers
    for k in range(0, nz, CHUNK):
        c = [levels_of(ref, k, CHUNK, rows) for ref in (coef_east, coef_north, coef_down)]
        changes = []
        for t in range(tracers):
            value = levels_of(field, t * nz + k, CHUNK, rows)
            below = levels_of(field, t * nz + k + CHUNK, 1, rows) if k + CHUNK < nz else zero[None]
            change, above[t] = laplacian(value, below, above[t], *c)
            changes.append(change)
            packed_field = packed_into(packed_field, value, t * nz + k, pair)
        for t in range(tracers):
            packed_image = packed_into(packed_image, changes[t], t * nz + k, pair)
        for t in range(tracers):
            put_levels(image, t * nz + k, changes[t])
    message[pl.ds(0, rows), :] = packed_image
    message[pl.ds(rows, rows), :] = packed_field
    message[pl.ds(2 * rows, rows), :] = for_tracers(packed_east, tracers, nz)

    even = is_even("lat")

    def edge(side):
        first = (rows - 1) * side
        out = [ref[pl.ds(first + t * nz * rows, nz, rows), :] for ref in (image, field) for t in range(tracers)]
        return out + [(east_own, north_own)[side][pl.ds(first, nz, rows), :]]

    for at, (south, north_) in enumerate(zip(edge(0), edge(1))):
        rows_a[pl.ds(at * nz, nz), :] = jnp.where(even, north_, south)
        rows_b[pl.ds(at * nz, nz), :] = jnp.where(even, south, north_)


def for_tracers(packed, tracers, nz):
    return sum((pltpu.roll(packed, 2 * nz * t, 1) for t in range(1, tracers)), packed)


def stacked(parts):
    lanes = parts[0].shape[1]
    row = iota((8, lanes), 0)
    total = jnp.zeros((8, lanes), F32)
    for i, part in enumerate(parts):
        total = jnp.where(row == i, part, total)
    return total


def folded(x):
    return sum(x[i : i + 8] for i in range(0, x.shape[0], 8))


def interior_kernel(tracers, nz, rows, field, image, coef_east, coef_north, coef_down, twice, packed, sums):
    lanes = field.shape[1]
    pair, last_lane = iota((rows, lanes), 1) >> 1, iota((CHUNK, rows, lanes), 2) == lanes - 1
    zero = jnp.zeros((rows, lanes), F32)
    packed_twice, packed_north, packed_down, packed_inner = [zero] * 4
    totals = [[zero] * 4 for _ in range(tracers)]
    above = [zero[None]] * tracers
    for k in range(0, nz, CHUNK):
        c = [levels_of(ref, k, CHUNK, rows) for ref in (coef_east, coef_north, coef_down)]
        results = []
        for t in range(tracers):
            w = levels_of(image, t * nz + k, CHUNK, rows)
            below = levels_of(image, t * nz + k + CHUNK, 1, rows) if k + CHUNK < nz else zero[None]
            y, above[t] = laplacian(w, below, above[t], *c)
            results.append(y)
            v = levels_of(field, t * nz + k, CHUNK, rows)
            for i, product in enumerate((v * v, v * w, w * w, w * y)):
                totals[t][i] = totals[t][i] + jnp.sum(product, axis=0)
        inner = jnp.where(last_lane, pltpu.roll(c[0], 1, 2), c[0])
        packed_north = packed_into(packed_north, c[1], k, pair)
        packed_down = packed_into(packed_down, c[2], k, pair)
        packed_inner = packed_into(packed_inner, inner, k, pair)
        for t in range(tracers):
            packed_twice = packed_into(packed_twice, results[t], t * nz + k, pair)
        for t in range(tracers):
            put_levels(twice, t * nz + k, results[t])
    packed[pl.ds(0, rows), :] = packed_twice
    for i, part in enumerate((packed_north, packed_down, packed_inner)):
        packed[pl.ds((i + 1) * rows, rows), :] = for_tracers(part, tracers, nz)
    for t in range(tracers):
        for i in range(4):
            sums[pl.ds((4 * t + i) * 8, 8), :] = folded(totals[t][i])


def sums_kernel(tracers, nz, rows, devices, image_in, twice_in, coef_east, coef_north, coef_down, rows_a, rows_b, got_rows_a,
                got_rows_b, own, got_a, got_b, packed, sums, image, twice, corrections, result):
    lanes = own.shape[1]
    even = is_even("lat")
    pair, level = iota((nz, lanes), 1) >> 1, iota((nz, lanes), 0)
    row = iota((rows, lanes), 0)
    north, down, inner = [packed[pl.ds((i + 1) * rows, rows), :] for i in range(3)]
    dots = [[jnp.zeros((8, lanes), F32) for _ in range(3)] for _ in range(tracers)]
    nothing = jnp.zeros((1, lanes), F32)
    row_change, row_inside = jnp.zeros((rows, lanes), F32), jnp.zeros((rows, lanes), F32)
    lat_coef, lat_ring, lat_change = [], [], []
    stores = []
    for side in range(SIDES):
        def part(at, a, b):
            first, second = (b, a) if side == 0 else (a, b)
            return jnp.where(even, first[pl.ds(at * nz, nz), :], second[pl.ds(at * nz, nz), :])

        own_row = lambda at: part(at, rows_a, rows_b)
        got_row = lambda at: part(at, got_rows_a, got_rows_b)
        own_coef, got_coef = own_row(2 * tracers), got_row(2 * tracers)
        c = got_coef * (own_coef > 0).astype(F32) if side == 0 else own_coef * (got_coef > 0).astype(F32)
        first, next_row, between = ((0, 1, 0), (rows - 1, rows - 2, rows - 2))[side]
        c_east, c_down = coef_east[pl.ds(first, nz, rows), :], coef_down[pl.ds(first, nz, rows), :]
        c_inner = coef_north[pl.ds(between, nz, rows), :]
        packed_coef, packed_ring, packed_e, packed_inside = [nothing] * 4
        for t in range(tracers):
            b, w = own_row(tracers + t), own_row(t)
            f = c * (got_row(tracers + t) - b)
            e = -f
            ring = got_row(t) + f
            flux_east = c_east * (pltpu.roll(e, lanes - 1, 1) - e)
            flux_down = c_down * (pltpu.roll(e, nz - 1, 0) - e)
            inside = (pltpu.roll(flux_east, 1, 1) - flux_east) + (pltpu.roll(flux_down, 1, 0) - flux_down) + c_inner * e
            changed = w + e
            through = c * (ring - changed)
            at = pl.ds(first + t * nz * rows, nz, rows)
            at_next = pl.ds(next_row + t * nz * rows, nz, rows)
            y = twice_in[at, :]
            stores.append((image, at, changed))
            stores.append((twice, at, y + inside - through))
            stores.append((twice, at_next, twice_in[at_next, :] - c_inner * e))
            for i, value in enumerate((b * e, (w + changed) * e, (2.0 * y + inside) * e - changed * through)):
                dots[t][i] = dots[t][i] + folded(value)
            packed_coef = packed_coef + spread(c, nz * t, pair, level)
            packed_ring = packed_ring + spread(ring, nz * t, pair, level)
            packed_e = packed_e + spread(e, nz * t, pair, level)
            packed_inside = packed_inside + spread(inside, nz * t, pair, level)
        row_change = jnp.where(row == first, packed_e, row_change)
        row_inside = jnp.where(row == first, packed_inside, row_inside)
        row_inside = jnp.where(row == next_row, -north[between : between + 1] * packed_e, row_inside)
        lat_coef.append(packed_coef)
        lat_ring.append(packed_ring)
        lat_change.append(-packed_e)
    for ref, at, value in stores:
        ref[at, :] = value

    even = is_even("lon")
    even_lane = (iota((rows, lanes), 1) & 1) == 0

    def neighbours(at):
        a, b = got_a[at, :], got_b[at, :]
        return from_neighbours(jnp.where(even, a, b), jnp.where(even, b, a), even_lane)

    parts = [pl.ds(i * rows, rows) for i in range(3)]
    own_image, own_field, own_east = [own[p, :] for p in parts]
    got_image, got_field, got_east = [neighbours(p) for p in parts]
    before = own_image + row_change
    y = packed[pl.ds(0, rows), :] + row_inside
    c = face(own_east, got_east, even_lane)
    f = c * (got_field - own_field)
    e = -f
    after = before + e
    ring = got_image + f
    through = c * (ring - after)
    through_new = through_old = halves = jnp.zeros((rows, lanes), F32)
    for side in range(SIDES):
        here = row == (rows - 1) * side
        through_new = jnp.where(here, lat_coef[side] * (lat_ring[side] - after), through_new)
        through_old = jnp.where(here, lat_coef[side] * (lat_ring[side] - before), through_old)
        halves = jnp.where(here, lat_coef[side] * lat_ring[side] * f + c * ring * lat_change[side], halves)
    flux_down = down * (pltpu.roll(e, lanes - 2, 1) - e)
    flux_north = north * (pltpu.roll(e, rows - 1, 0) - e)
    inside = (pltpu.roll(flux_down, 2, 1) - flux_down) + (pltpu.roll(flux_north, 1, 0) - flux_north) + inner * e
    beside = -inner * e
    corrections[parts[0], :] = e
    corrections[parts[1], :] = inside - through - (through_new - through_old)
    corrections[parts[2], :] = jnp.where(even_lane, beside, pltpu.roll(beside, 2, 1))
    edges = [(rows - 1) * side for side in range(SIDES)]
    corrections[pl.ds(3 * rows, 8), :] = stacked(lat_coef + [c[i : i + 1] for i in edges])

    column_dots = [folded(value) for value in (
        own_field * e,
        (before + after) * e,
        (2.0 * y + inside) * e - after * (through + through_new) + before * through_old + halves,
    )]
    tile_lane, tile_row = iota((8, lanes), 1), iota((8, lanes), 0)
    total = jnp.zeros((8, lanes), F32)
    for t in range(tracers):
        mine = (tile_lane >= 2 * nz * t) & (tile_lane < 2 * nz * (t + 1))
        for i in range(4):
            value = sums[pl.ds((4 * t + i) * 8, 8), :]
            if i:
                value = value + dots[t][i - 1] + jnp.where(mine, column_dots[i - 1], 0.0)
            total = jnp.where(tile_row == 4 * t + i, jnp.sum(value, axis=0, keepdims=True), total)
    total = jnp.sum(total, axis=1, keepdims=True)
    total = jnp.sum(jnp.where(tile_row == tile_lane, total, 0.0), axis=0, keepdims=True)
    even_row = (iota((1, lanes), 1) & 1) == 0
    south, north_ = edges
    shares = [total, 2.0 * lat_coef[1] * f[north_ : north_ + 1], f[south : south + 1]]
    shares += [jnp.where(even_row, 2.0 * c[i : i + 1] * part, part) for i, part in zip(edges, lat_change)]
    tile = stacked(shares)
    for i in range(devices):
        result[pl.ds(8 * i, 8), :] = tile


def finish_kernel(tracers, nz, rows, devices, field, image, twice, corrections, sums, solution_out, residual_out,
                  solution, residual, sems):
    lanes = field.shape[1]
    across, along = lax.axis_size("lon"), lax.axis_size("lat")
    one, tile_row, tile_lane = iota((1, lanes), 1), iota((8, lanes), 0), iota((8, lanes), 1)
    total = cross_lat = cross_lon = jnp.zeros((8, lanes), F32)
    tiles = lambda i: sums[pl.ds(8 * along * i, 8 * along), :].reshape(along, 8, lanes)
    for i in range(across):
        here, there = tiles(i), tiles((i + 1) % across)
        total = total + jnp.sum(here, axis=0)
        cross_lat = cross_lat + jnp.sum(here[:-1] * pltpu.roll(here[1:], 7, 1), axis=0)
        cross_lon = cross_lon + jnp.sum(here * pltpu.roll(there, lanes - 1, 2), axis=0)
    even_tile = (tile_lane & 1) == 0
    lon_rows = (tile_row == 3) | (tile_row == 4)
    cross = jnp.where(tile_row == 1, cross_lat, jnp.where(lon_rows & even_tile, cross_lon, 0.0))

    lon, lat = lax.axis_index("lon"), lax.axis_index("lat")
    tile = lambda i, j: sums[pl.ds(pl.multiple_of(8 * (i * along + j), 8), 8), :]
    south = tile(lon, jnp.maximum(lat - 1, 0)) * jnp.where(lat > 0, 0.5, 0.0)
    north = tile(lon, jnp.minimum(lat + 1, along - 1))
    east = tile(lax.rem(lon + 1, across), lat)
    west = tile(lax.rem(lon + across - 1, across), lat)
    faces = corrections[pl.ds(3 * rows, 8), :]
    beyond = from_neighbours(east, 0.5 * west, even_tile)
    even_one = (one & 1) == 0
    sides = []
    for side in range(SIDES):
        along_lat = south[1:2] if side == 0 else faces[1:2] * north[2:3]
        part = beyond[3 + side : 4 + side]
        sides.append(along_lat + jnp.where(even_one, faces[2 + side : 3 + side] * part, part))
    row = iota((rows, lanes), 0)
    e, change, beside = [corrections[pl.ds(i * rows, rows), :] for i in range(3)]
    change = change + jnp.where(row == 0, sides[0], jnp.where(row == rows - 1, sides[1], 0.0))

    lane = iota((CHUNK, rows, lanes), 2)
    edge = (lane == 0) | (lane == lanes - 1)
    inner = (lane == 1) | (lane == lanes - 2)
    cross = jnp.sum(cross, axis=0, keepdims=True)

    def number(i):
        return jnp.sum(jnp.where(one == i, total[:1], 0.0), axis=1, keepdims=True)

    copies = []
    for t in range(tracers):
        bb, bw, ww, wy = [number(4 * t + i) for i in range(4)]
        mine = (one >= 2 * nz * t) & (one < 2 * nz * (t + 1))
        wy = wy - jnp.sum(jnp.where(mine, cross, 0.0), axis=1, keepdims=True)
        whole = bb + bw
        step = bb / whole
        rest = bw / whole
        new = rest * rest * bb - 2.0 * rest * step * bw + step * step * ww
        beta = new / bb
        tau = beta + rest
        step_next = new / (new + beta * beta * bb + tau * tau * bw - 2.0 * tau * step * ww + step * step * wy)
        both = step * step_next
        s_b = step + step_next * tau
        r_b = rest - step_next * tau
        r_w = both - step - step_next * tau
        s_edge = -both * e
        r_edge = r_w * e + both * change
        r_inner = both * beside
        for slot in range(t * nz, (t + 1) * nz, CHUNK):
            v, w, y = [levels_of(ref, slot, CHUNK, rows) for ref in (field, image, twice)]
            more = jnp.where(edge, unpacked(s_edge, slot, CHUNK), 0.0)
            much = jnp.where(inner, unpacked(r_inner, slot, CHUNK, 2), 0.0)
            much = jnp.where(edge, unpacked(r_edge, slot, CHUNK), much)
            put_levels(solution, slot, (s_b * v - both * w) + more)
            put_levels(residual, slot, (r_b * v + r_w * w + both * y) + much)
            at = pl.ds(slot * rows, CHUNK * rows)
            for a, b in ((solution, solution_out), (residual, residual_out)):
                copy = pltpu.make_async_copy(a.at[at], b.at[at], sems.at[len(copies)])
                copy.start()
                copies.append(copy)
    for copy in copies:
        copy.wait()


def swaps(devices, second, periodic):
    pairs = []
    for i in range(devices):
        j = i + 1 if (i % 2 == 0) != second else i - 1
        if periodic or 0 <= j < devices:
            pairs.append((i, j % devices))
    return pairs


def swapped(x, axis, second, periodic):
    return lax.ppermute(x, axis, swaps(lax.axis_size(axis), second, periodic))


def body(right_side, sea_mask, levels, east_diffusivity, north_diffusivity, vertical_diffusivity):
    tracers, nz, rows, lanes = right_side.shape
    devices = lax.axis_size("lon") * lax.axis_size("lat")
    flat = lambda x: x.reshape(-1, lanes)
    outside = lambda x: pltpu.with_memory_space_constraint(flat(x), pltpu.HBM)
    n = nz * rows
    cells = tracers * n * lanes

    def call(kernel, outs, flops, space=pltpu.VMEM, **more):
        cost = pl.CostEstimate(flops=flops, bytes_accessed=4 * lanes * sum(outs), transcendentals=0)
        return pl.pallas_call(
            functools.partial(kernel, tracers, nz, rows),
            out_shape=[space((m, lanes), F32) for m in outs],
            compiler_params=pltpu.CompilerParams(vmem_limit_bytes=32 * 1024 * 1024),
            cost_estimate=cost,
            **more,
        )

    def with_devices(kernel):
        return lambda tracers, nz, rows, *refs: kernel(tracers, nz, rows, devices, *refs)

    scratch = lambda m, dtype: pltpu.VMEM((m, lanes), dtype)
    field, coef_east, coef_north, coef_down, image, message, rows_a, rows_b = call(
        prepare_kernel,
        [tracers * n, n, n, n, tracers * n, 3 * rows, FIELDS * nz, FIELDS * nz],
        60 * cells,
        in_specs=[pl.BlockSpec(memory_space=pltpu.HBM)] * 6,
        scratch_shapes=[scratch(n, jnp.int32), scratch(rows, jnp.int32)] + [scratch(n, jnp.bfloat16)] * 3
        + [scratch(n, F32)] * 2 + [pltpu.SemaphoreType.DMA((6,))],
        name="prepare",
    )(*map(outside, (right_side, sea_mask, levels, east_diffusivity, north_diffusivity, vertical_diffusivity)))
    got_b = swapped(message, "lon", True, True)
    got_a = swapped(message, "lon", False, True)
    got_rows_b = swapped(rows_b, "lat", True, False)
    got_rows_a = swapped(rows_a, "lat", False, False)
    coefs = (coef_east, coef_north, coef_down)
    twice, packed, sums = call(interior_kernel, [tracers * n, 4 * rows, 8 * 4 * tracers], 60 * cells, name="interior")(
        field, image, *coefs)
    image, twice, corrections, sums = call(
        with_devices(sums_kernel), [tracers * n, tracers * n, 3 * rows + 8, 8 * devices], cells,
        input_output_aliases={0: 0, 1: 1}, name="sums",
    )(image, twice, *coefs, rows_a, rows_b, got_rows_a, got_rows_b, message, got_a, got_b, packed, sums)
    sums = lax.all_to_all(sums, ("lon", "lat"), 0, 0, tiled=True)
    copies = 2 * tracers * nz // CHUNK
    solution_field, residual = call(
        with_devices(finish_kernel), [tracers * n] * 2, 20 * cells, space=jax.ShapeDtypeStruct,
        out_specs=[pl.BlockSpec(memory_space=pltpu.HBM)] * 2,
        scratch_shapes=[scratch(tracers * n, F32)] * 2 + [pltpu.SemaphoreType.DMA((copies,))],
        name="finish",
    )(field, image, twice, corrections, sums)
    return solution_field.reshape(right_side.shape), residual.reshape(right_side.shape)


def solution(mesh):
    return jax.shard_map(
        body,
        mesh=mesh,
        in_specs=(
            P(None, None, "lat", "lon"),
            P(None, "lat", "lon"),
            P("lat", "lon"),
            P(None, "lat", "lon"),
            P(None, "lat", "lon"),
            P(None, "lat", "lon"),
        ),
        out_specs=(P(None, None, "lat", "lon"), P(None, None, "lat", "lon")),
        check_vma=False,
    )
```

time: 31.5 us -> 29.9 us (0.949)
  blocking collectives: 15.2 us -> 13.9 us
  Pallas kernels: 6.13 us -> 5.72 us
    all_to_all x1, blocking collectives: 15.2 us -> 13.9 us  [body(): sums = lax.all_to_all(sums, ('lon', 'lat'), 0, 0, tiled=True)]
    pallas_call x6 -> x4, Pallas kernels: 6.13 us -> 5.72 us  [the longest x1 2.46 us: body(): call(prepare_kernel, [tracers * n, n, n, n, tracers * n, 3 * rows, FIELDS...]
  transfers between devices with their start and end apart: 4 -> 4, of which waited for: 2 -> 2; matrix products, arithmetic and copies ran while one was open for 0% -> 0% of each run, Pallas kernels for 8% -> 4%
where the time goes in v2:
time: 29.9 us; the launch traced here: 29.7 us
  blocking collectives  13.9 us (46%)
  starting transfers between devices  6.79 us (23%)
  Pallas kernels  5.72 us (19%)
  waiting for transfers between devices  2.59 us (9%)
  between operations  0.66 us (2%)
    all_to_all x1, blocking collectives, body(): sums = lax.all_to_all(sums, ('lon', 'lat'), 0, 0, tiled=True)  13.9 us
    ppermute x4, starting transfers between devices, swapped(): return lax.ppermute(x, axis, swaps(lax.axis_size(axis), second, periodic))  6.79 us
    ppermute x4, waiting for transfers between devices, swapped(): return lax.ppermute(x, axis, swaps(lax.axis_size(axis), second, periodic))  2.59 us
    pallas_call x1, Pallas kernels, body(): call(prepare_kernel, [tracers * n, n, n, n, tracers * n, 3 * rows, FIELDS...  2.46 us
    pallas_call x1, Pallas kernels, body(): call(with_devices(finish_kernel), [tracers * n] * 2, 20 * cells, space=ja...  1.58 us
    pallas_call x1, Pallas kernels, body(): call(interior_kernel, [tracers * n, 4 * rows, 8 * 4 * tracers], 60 * cell...  1.24 us
  transfers between devices with their start and end apart: 4, of which 2 were waited for; matrix products, arithmetic and copies ran while one was open for 0% of the time, Pallas kernels for 4%

profile of v2, /device:TPU:0, one launch (start us, length us, event | category | flops | bytes accessed | tf_op | source)
XLA Modules:
  0.0 29.7 jit_solution(14330773956584526802)
XLA Ops:
  0.6 2.5 %prepare.1 = (f32[1024,128]{1,0:T(8,128)S(1)}, f32[512,128]{1,0:T(8,128)S(1)}, f32[512,128]{1,0:T(8,128)S(1)}, f32[512,128]{1,0:T(8,128)S(1)}, f32[1024,128]{1,0...) custom-call(f32[1024,128]{1,0:T(8,128)} %bitcast.11, s32[512,128]{1,0:T(8,128)} %bitcast.12, ...), custom_call_target="tpu_custom_call" | custom-call | flops 7864320 | bytes 2023424 | tf_op jit(solution)/shard_map/prepare/pallas_call | solution.py:413
  3.1 0.5 %collective-permute-start = (f32[160,128]{1,0:T(8,128)S(1)}, f32[160,128]{1,0:T(8,128)S(1)}, u32[]{:S(2)}, u32[]{:S(2)}) collective-permute-start(f32[160,128]{1,0:T(8,128)S(1)} %get-tuple-element.25.refs_5_), channel_id=1, source_target_pairs={{0,1},{1,0},{2,3},{3,2},{4,5},{5,4},{6,7},{7,6},{8,9},{9,8},{10,11... | collective-permute-start | bytes 245768 | tf_op jit(solution)/shard_map/ppermute | solution.py:388
  3.6 0.7 %collective-permute-start.1 = (f32[160,128]{1,0:T(8,128)S(1)}, f32[160,128]{1,0:T(8,128)S(1)}, u32[]{:S(2)}, u32[]{:S(2)}) collective-permute-start(f32[160,128]{1,0:T(8,128)S(1)} %get-tuple-element.26.refs_6_), channel_id=1, source_target_pairs={{1,2},{2,1},{5,6},{6,5},{9,10},{10,9},{13,14},{14,13},{17,18},{18,... | collective-permute-start | bytes 245768 | tf_op jit(solution)/shard_map/ppermute | solution.py:388
  4.3 5.6 %collective-permute-start.3 = (f32[48,128]{1,0:T(8,128)S(1)}, f32[48,128]{1,0:T(8,128)S(1)}, u32[]{:S(2)}, u32[]{:S(2)}) collective-permute-start(f32[48,128]{1,0:T(8,128)S(1)} %get-tuple-element.27.refs_9_), channel_id=1, source_target_pairs={{0,28},{4,8},{8,4},{12,16},{16,12},{20,24},{24,20},{28,0},{1,29},{... | collective-permute-start | bytes 73736 | tf_op jit(solution)/shard_map/ppermute | solution.py:388
  9.9 0.0 collective-permute-start.2
  9.9 1.2 %interior.1 = (f32[1024,128]{1,0:T(8,128)S(1)}, f32[64,128]{1,0:T(8,128)S(1)}, f32[64,128]{1,0:T(8,128)S(1)}) custom-call(f32[1024,128]{1,0:T(8,128)S(1)} %get-tuple-element.19.field.refs_0_, f32[1024,128]{1,0:T(8,128)S(1)} %get-tuple-element.20.image.refs_0_, f32[512,128]{1,0:T(8,128)S(1)} %get-tuple-element.21.coef_east.refs_2_, ...), custom_call_target="tpu_custom_call" | custom-call | flops 7864320 | bytes 589824 | tf_op jit(solution)/shard_map/interior/pallas_call | solution.py:427
  11.1 0.6 %collective-permute-done.3.refs_11_ = f32[48,128]{1,0:T(8,128)S(1)} collective-permute-done((f32[48,128]{1,0:T(8,128)S(1)}, f32[48,128]{1,0:T(8,128)S(1)}, u32[]{:S(2)}, u32[]{:S(2)}) %collective-permute-start.3) | collective-permute-done | bytes 24608 | tf_op jit(solution)/shard_map/ppermute | solution.py:388
  11.7 2.0 %collective-permute-done.2.refs_10_ = f32[48,128]{1,0:T(8,128)S(1)} collective-permute-done((f32[48,128]{1,0:T(8,128)S(1)}, f32[48,128]{1,0:T(8,128)S(1)}, u32[]{:S(2)}, u32[]{:S(2)}) %collective-permute-start.2) | collective-permute-done | bytes 24608 | tf_op jit(solution)/shard_map/ppermute | solution.py:388
  13.7 0.0 collective-permute-done.refs_7_
  13.7 0.0 collective-permute-done.1.refs_8_
  13.7 0.4 %sums.1 = (f32[1024,128]{1,0:T(8,128)S(1)}, f32[1024,128]{1,0:T(8,128)S(1)}, f32[56,128]{1,0:T(8,128)S(1)}, f32[256,128]{1,0:T(8,128)S(1)}) custom-call(f32[1024,128]{1,0:T(8,128)S(1)} %get-tuple-element.20.image.refs_0_, f32[1024,128]{1,0:T(8,128)S(1)} %get-tuple-element.24.refs_1_, ...), custom_call_target="tpu_custom_call", output_to_operand_aliasing={{0}: (0, {}), {1}: (1, {})} | custom-call | flops 131072 | bytes 1208320 | tf_op jit(solution)/shard_map/sums/pallas_call | solution.py:429
  14.2 13.9 %all_to_all.11 = f32[32,8,128]{2,1,0:T(8,128)S(1)} all-to-all(f32[32,8,128]{2,1,0:T(8,128)S(1)} %bitcast.10), channel_id=1, replica_groups=mesh['lon'=8,'lat'=4] {'lon','lat'}, dimensions={0} | all-to-all | bytes 262144 | tf_op jit(solution)/shard_map/all_to_all | solution.py:433
  28.1 1.6 %finish.1 = (f32[1024,128]{1,0:T(8,128)}, f32[1024,128]{1,0:T(8,128)}) custom-call(f32[1024,128]{1,0:T(8,128)S(1)} %get-tuple-element.19.field.refs_0_, f32[1024,128]{1,0:T(8,128)S(1)} %get-tuple-element.30.refs_1_, f32[1024,128]{1,0:T(8,128)S(1)} %get-tuple-element.31.refs_2_, f32[56,128]{1,0:T(8,128)S(1)} %get-tuple-element.32.refs_3_, f32[256,128]{1,0:T(8,128)S(1)} %bitcast.9), custom_call_target="tpu_custom_call" | custom-call | flops 2621440 | bytes 1048576 | tf_op jit(solution)/shard_map/finish/pallas_call | solution.py:435
Async XLA Ops:
  3.1 10.6 %collective-permute-start = (f32[160,128]{1,0:T(8,128)S(1)}, f32[160,128]{1,0:T(8,128)S(1)}, u32[]{:S(2)}, u32[]{:S(2)}) collective-permute-start(f32[160,128]{1,0:T(8,128)S(1)} %get-tuple-element.25.refs_5_), channel_id=1, source_target_pairs={{0,1},{1,0},{2,3},{3,2},{4,5},{5,4},{6,7},{7,6},{8,9},{9,8},{10,11... | collective-permute-start | bytes 245768 | tf_op jit(solution)/shard_map/ppermute | solution.py:388
  3.6 10.1 %collective-permute-start.1 = (f32[160,128]{1,0:T(8,128)S(1)}, f32[160,128]{1,0:T(8,128)S(1)}, u32[]{:S(2)}, u32[]{:S(2)}) collective-permute-start(f32[160,128]{1,0:T(8,128)S(1)} %get-tuple-element.26.refs_6_), channel_id=1, source_target_pairs={{1,2},{2,1},{5,6},{6,5},{9,10},{10,9},{13,14},{14,13},{17,18},{18,... | collective-permute-start | bytes 245768 | tf_op jit(solution)/shard_map/ppermute | solution.py:388
  4.3 7.4 %collective-permute-start.3 = (f32[48,128]{1,0:T(8,128)S(1)}, f32[48,128]{1,0:T(8,128)S(1)}, u32[]{:S(2)}, u32[]{:S(2)}) collective-permute-start(f32[48,128]{1,0:T(8,128)S(1)} %get-tuple-element.27.refs_9_), channel_id=1, source_target_pairs={{0,28},{4,8},{8,4},{12,16},{16,12},{20,24},{24,20},{28,0},{1,29},{... | collective-permute-start | bytes 73736 | tf_op jit(solution)/shard_map/ppermute | solution.py:388
  9.9 3.8 %collective-permute-start.2 = (f32[48,128]{1,0:T(8,128)S(1)}, f32[48,128]{1,0:T(8,128)S(1)}, u32[]{:S(2)}, u32[]{:S(2)}) collective-permute-start(f32[48,128]{1,0:T(8,128)S(1)} %get-tuple-element.27.refs_9_), channel_id=1, source_target_pairs={{0,4},{4,0},{8,12},{12,8},{16,20},{20,16},{24,28},{28,24},{1,5},{5... | collective-permute-start | bytes 73736 | tf_op jit(solution)/shard_map/ppermute | solution.py:388

commit v3 on v2

--- a/solution.py
+++ b/solution.py
@@ -9,6 +9,7 @@
 
 F32 = jnp.float32
 CHUNK = 8
+SHARES = 5
 SIDES = 2
 FIELDS = 5
 
@@ -66,8 +67,8 @@
 
 
 def prepare_kernel(tracers, nz, rows, field_in, mask_in, levels_in, east_in, north_in, down_in,
-                   field, coef_east, coef_north, coef_down, image, message, rows_a, rows_b,
-                   mask, levels, east, north, down, east_own, north_own, sems):
+                   field, coef_east, coef_north, coef_down, east_own, north_own, image, message,
+                   mask, levels, east, north, down, sems):
     copies = [
         pltpu.make_async_copy(a, b, sems.at[i])
         for i, (a, b) in enumerate(((levels_in, levels), (mask_in, mask), (east_in, east), (north_in, north),
@@ -120,16 +121,26 @@
     message[pl.ds(rows, rows), :] = packed_field
     message[pl.ds(2 * rows, rows), :] = for_tracers(packed_east, tracers, nz)
 
-    even = is_even("lat")
+
+def edge_rows(tracers, nz, rows, field, image, east_own, north_own, second, out):
+    southern = is_even("lat") if second else jnp.logical_not(is_even("lat"))
 
     def edge(side):
         first = (rows - 1) * side
-        out = [ref[pl.ds(first + t * nz * rows, nz, rows), :] for ref in (image, field) for t in range(tracers)]
-        return out + [(east_own, north_own)[side][pl.ds(first, nz, rows), :]]
+        parts = [ref[pl.ds(first + t * nz * rows, nz, rows), :] for ref in (image, field) for t in range(tracers)]
+        return parts + [(east_own, north_own)[side][pl.ds(first, nz, rows), :]]
 
     for at, (south, north_) in enumerate(zip(edge(0), edge(1))):
-        rows_a[pl.ds(at * nz, nz), :] = jnp.where(even, north_, south)
-        rows_b[pl.ds(at * nz, nz), :] = jnp.where(even, south, north_)
+        out[pl.ds(at * nz, nz), :] = jnp.where(southern, south, north_)
+
+
+def edges_kernel(tracers, nz, rows, field, image, east_own, north_own, rows_b):
+    edge_rows(tracers, nz, rows, field, image, east_own, north_own, True, rows_b)
+
+
+def later_kernel(tracers, nz, rows, field, image, east_own, north_own, message, rows_b, rows_a, message_a):
+    edge_rows(tracers, nz, rows, field, image, east_own, north_own, False, rows_a)
+    message_a[...] = message[...]
 
 
 def for_tracers(packed, tracers, nz):
@@ -293,41 +304,36 @@
     south, north_ = edges
     shares = [total, 2.0 * lat_coef[1] * f[north_ : north_ + 1], f[south : south + 1]]
     shares += [jnp.where(even_row, 2.0 * c[i : i + 1] * part, part) for i, part in zip(edges, lat_change)]
-    tile = stacked(shares)
-    for i in range(devices):
-        result[pl.ds(8 * i, 8), :] = tile
+    for i, share in enumerate(shares):
+        result[pl.ds(i, devices, SHARES), :] = jnp.broadcast_to(share, (devices, lanes))
 
 
 def finish_kernel(tracers, nz, rows, devices, field, image, twice, corrections, sums, solution_out, residual_out,
                   solution, residual, sems):
     lanes = field.shape[1]
     across, along = lax.axis_size("lon"), lax.axis_size("lat")
-    one, tile_row, tile_lane = iota((1, lanes), 1), iota((8, lanes), 0), iota((8, lanes), 1)
-    total = cross_lat = cross_lon = jnp.zeros((8, lanes), F32)
-    tiles = lambda i: sums[pl.ds(8 * along * i, 8 * along), :].reshape(along, 8, lanes)
-    for i in range(across):
-        here, there = tiles(i), tiles((i + 1) % across)
-        total = total + jnp.sum(here, axis=0)
-        cross_lat = cross_lat + jnp.sum(here[:-1] * pltpu.roll(here[1:], 7, 1), axis=0)
-        cross_lon = cross_lon + jnp.sum(here * pltpu.roll(there, lanes - 1, 2), axis=0)
-    even_tile = (tile_lane & 1) == 0
-    lon_rows = (tile_row == 3) | (tile_row == 4)
-    cross = jnp.where(tile_row == 1, cross_lat, jnp.where(lon_rows & even_tile, cross_lon, 0.0))
+    one = iota((1, lanes), 1)
+    even_one = (one & 1) == 0
+    total, to_north, to_south, lon_south, lon_north = [sums[pl.ds(i, devices, SHARES), :] for i in range(SHARES)]
+    total = jnp.sum(total, axis=0, keepdims=True)
+    device, lane_of = iota((devices, lanes), 0), iota((devices, lanes), 1)
+    cross = jnp.where(lax.rem(device, along) < along - 1, to_north * pltpu.roll(to_south, devices - 1, 0), 0.0)
+    for part in (lon_south, lon_north):
+        beyond = pltpu.roll(pltpu.roll(part, devices - along, 0), lanes - 1, 1)
+        cross = cross + jnp.where((lane_of & 1) == 0, part * beyond, 0.0)
+    cross = jnp.sum(cross, axis=0, keepdims=True)
 
     lon, lat = lax.axis_index("lon"), lax.axis_index("lat")
-    tile = lambda i, j: sums[pl.ds(pl.multiple_of(8 * (i * along + j), 8), 8), :]
-    south = tile(lon, jnp.maximum(lat - 1, 0)) * jnp.where(lat > 0, 0.5, 0.0)
-    north = tile(lon, jnp.minimum(lat + 1, along - 1))
-    east = tile(lax.rem(lon + 1, across), lat)
-    west = tile(lax.rem(lon + across - 1, across), lat)
+    share = lambda i, j, at: sums[pl.ds(SHARES * (i * along + j) + at, 1), :]
     faces = corrections[pl.ds(3 * rows, 8), :]
-    beyond = from_neighbours(east, 0.5 * west, even_tile)
-    even_one = (one & 1) == 0
+    lat_sides = (share(lon, jnp.maximum(lat - 1, 0), 1) * jnp.where(lat > 0, 0.5, 0.0),
+                 share(lon, jnp.minimum(lat + 1, along - 1), 2) * faces[1:2])
     sides = []
     for side in range(SIDES):
-        along_lat = south[1:2] if side == 0 else faces[1:2] * north[2:3]
-        part = beyond[3 + side : 4 + side]
-        sides.append(along_lat + jnp.where(even_one, faces[2 + side : 3 + side] * part, part))
+        east = share(lax.rem(lon + 1, across), lat, 3 + side)
+        west = share(lax.rem(lon + across - 1, across), lat, 3 + side)
+        part = from_neighbours(east, 0.5 * west, even_one)
+        sides.append(lat_sides[side] + jnp.where(even_one, faces[2 + side : 3 + side] * part, part))
     row = iota((rows, lanes), 0)
     e, change, beside = [corrections[pl.ds(i * rows, rows), :] for i in range(3)]
     change = change + jnp.where(row == 0, sides[0], jnp.where(row == rows - 1, sides[1], 0.0))
@@ -335,10 +341,9 @@
     lane = iota((CHUNK, rows, lanes), 2)
     edge = (lane == 0) | (lane == lanes - 1)
     inner = (lane == 1) | (lane == lanes - 2)
-    cross = jnp.sum(cross, axis=0, keepdims=True)
 
     def number(i):
-        return jnp.sum(jnp.where(one == i, total[:1], 0.0), axis=1, keepdims=True)
+        return jnp.sum(jnp.where(one == i, total, 0.0), axis=1, keepdims=True)
 
     copies = []
     for t in range(tracers):
@@ -410,27 +415,31 @@
         return lambda tracers, nz, rows, *refs: kernel(tracers, nz, rows, devices, *refs)
 
     scratch = lambda m, dtype: pltpu.VMEM((m, lanes), dtype)
-    field, coef_east, coef_north, coef_down, image, message, rows_a, rows_b = call(
+    field, coef_east, coef_north, coef_down, east_own, north_own, image, message = call(
         prepare_kernel,
-        [tracers * n, n, n, n, tracers * n, 3 * rows, FIELDS * nz, FIELDS * nz],
+        [tracers * n] + [n] * 5 + [tracers * n, 3 * rows],
         60 * cells,
         in_specs=[pl.BlockSpec(memory_space=pltpu.HBM)] * 6,
         scratch_shapes=[scratch(n, jnp.int32), scratch(rows, jnp.int32)] + [scratch(n, jnp.bfloat16)] * 3
-        + [scratch(n, F32)] * 2 + [pltpu.SemaphoreType.DMA((6,))],
+        + [pltpu.SemaphoreType.DMA((6,))],
         name="prepare",
     )(*map(outside, (right_side, sea_mask, levels, east_diffusivity, north_diffusivity, vertical_diffusivity)))
     got_b = swapped(message, "lon", True, True)
-    got_a = swapped(message, "lon", False, True)
+    rows_b, = call(edges_kernel, [FIELDS * nz], cells, name="edges")(field, image, east_own, north_own)
     got_rows_b = swapped(rows_b, "lat", True, False)
+    coefs = (coef_east, coef_north, coef_down)
+    rows_a, message_a = call(later_kernel, [FIELDS * nz, 3 * rows], cells, name="later")(
+        field, image, east_own, north_own, message, rows_b)
+    twice, packed, sums = call(
+        interior_kernel, [tracers * n, 4 * rows, 8 * 4 * tracers], 60000 * cells, name="interior"
+    )(field, image, *coefs)
+    got_a = swapped(message_a, "lon", False, True)
     got_rows_a = swapped(rows_a, "lat", False, False)
-    coefs = (coef_east, coef_north, coef_down)
-    twice, packed, sums = call(interior_kernel, [tracers * n, 4 * rows, 8 * 4 * tracers], 60 * cells, name="interior")(
-        field, image, *coefs)
     image, twice, corrections, sums = call(
-        with_devices(sums_kernel), [tracers * n, tracers * n, 3 * rows + 8, 8 * devices], cells,
+        with_devices(sums_kernel), [tracers * n, tracers * n, 3 * rows + 8, SHARES * devices], cells,
         input_output_aliases={0: 0, 1: 1}, name="sums",
     )(image, twice, *coefs, rows_a, rows_b, got_rows_a, got_rows_b, message, got_a, got_b, packed, sums)
-    sums = lax.all_to_all(sums, ("lon", "lat"), 0, 0, tiled=True)
+    sums = lax.all_to_all(sums.reshape(devices, 1, -1), ("lon", "lat"), 0, 0, tiled=True).reshape(-1, lanes)
     copies = 2 * tracers * nz // CHUNK
     solution_field, residual = call(
         with_devices(finish_kernel), [tracers * n] * 2, 20 * cells, space=jax.ShapeDtypeStruct,

time: 29.9 us -> 26.6 us (0.89)
  blocking collectives: 13.9 us -> 10.2 us
  starting transfers between devices: 6.79 us -> 9.72 us
  waiting for transfers between devices: 2.59 us -> 0.01 us
    all_to_all x1, blocking collectives: 13.9 us -> 10.2 us  [body(): lax.all_to_all(sums.reshape(devices, 1, -1), ('lon', 'lat'), 0, 0, tiled=...]
    ppermute x4, starting transfers between devices: 6.79 us -> 9.72 us  [swapped(): return lax.ppermute(x, axis, swaps(lax.axis_size(axis), second, periodic))]
    ppermute x4, waiting for transfers between devices: 2.59 us -> 0.01 us  [swapped(): return lax.ppermute(x, axis, swaps(lax.axis_size(axis), second, periodic))]
    pallas_call x2 -> x4, Pallas kernels: 3.7 us -> 3.74 us  [the longest x1 2.41 us: body(): call(prepare_kernel, [tracers * n] + [n] * 5 + [tracers * n, 3 * rows], 6...]
  transfers between devices with their start and end apart: 4 -> 4, of which waited for: 2 -> 0; matrix products, arithmetic and copies ran while one was open for 0% -> 0% of each run, Pallas kernels for 4% -> 5%
where the time goes in v3:
time: 26.6 us; the launch traced here: 26.3 us
  blocking collectives  10.2 us (38%)
  starting transfers between devices  9.72 us (37%)
  Pallas kernels  5.72 us (22%)
  between operations  0.7 us (3%)
    all_to_all x1, blocking collectives, body(): lax.all_to_all(sums.reshape(devices, 1, -1), ('lon', 'lat'), 0, 0, tiled=...  10.2 us
    ppermute x4, starting transfers between devices, swapped(): return lax.ppermute(x, axis, swaps(lax.axis_size(axis), second, periodic))  9.72 us
    pallas_call x1, Pallas kernels, body(): call(prepare_kernel, [tracers * n] + [n] * 5 + [tracers * n, 3 * rows], 6...  2.41 us
    pallas_call x1, Pallas kernels, body(): call(with_devices(finish_kernel), [tracers * n] * 2, 20 * cells, space=ja...  1.54 us
    pallas_call x1, Pallas kernels, body(): call(interior_kernel, [tracers * n, 4 * rows, 8 * 4 * tracers], 60000 * c...  1.23 us
  transfers between devices with their start and end apart: 4, of which 0 were waited for; matrix products, arithmetic and copies ran while one was open for 0% of the time, Pallas kernels for 5%

profile of v3, /device:TPU:0, one launch (start us, length us, event | category | flops | bytes accessed | tf_op | source)
XLA Modules:
  0.0 26.3 jit_solution(12064357411236556128)
XLA Ops:
  0.6 2.4 %prepare.1 = (f32[1024,128]{1,0:T(8,128)S(1)}, f32[512,128]{1,0:T(8,128)S(1)}, f32[512,128]{1,0:T(8,128)S(1)}, f32[512,128]{1,0:T(8,128)S(1)}, f32[512,128]{1,0:...) custom-call(f32[1024,128]{1,0:T(8,128)} %bitcast.11, s32[512,128]{1,0:T(8,128)} %bitcast.12, ...), custom_call_target="tpu_custom_call" | custom-call | flops 7864320 | bytes 2383872 | tf_op jit(solution)/shard_map/prepare/pallas_call | solution.py:418
  3.0 6.0 %collective-permute-start.3 = (f32[48,128]{1,0:T(8,128)S(1)}, f32[48,128]{1,0:T(8,128)S(1)}, u32[]{:S(2)}, u32[]{:S(2)}) collective-permute-start(f32[48,128]{1,0:T(8,128)S(1)} %get-tuple-element.29.message.refs_9_), channel_id=1, source_target_pairs={{0,28},{4,8},{8,4},{12,16},{16,12},{20,24},{24,20},{28,0},{1,29},{... | collective-permute-start | bytes 73736 | tf_op jit(solution)/shard_map/ppermute | solution.py:393
  9.1 0.1 edges.1.rows_b.refs_6_
  9.1 0.7 %collective-permute-start.1 = (f32[160,128]{1,0:T(8,128)S(1)}, f32[160,128]{1,0:T(8,128)S(1)}, u32[]{:S(2)}, u32[]{:S(2)}) collective-permute-start(f32[160,128]{1,0:T(8,128)S(1)} %edges.1.rows_b.refs_6_), channel_id=1, source_target_pairs={{1,2},{2,1},{5,6},{6,5},{9,10},{10,9},{13,14},{14,13},{17,18},{18,... | collective-permute-start | bytes 245768 | tf_op jit(solution)/shard_map/ppermute | solution.py:393
  9.8 0.1 later.1
  9.9 0.1 collective-permute-start.2
  10.0 2.9 %collective-permute-start = (f32[160,128]{1,0:T(8,128)S(1)}, f32[160,128]{1,0:T(8,128)S(1)}, u32[]{:S(2)}, u32[]{:S(2)}) collective-permute-start(f32[160,128]{1,0:T(8,128)S(1)} %get-tuple-element.30.refs_5_), channel_id=1, source_target_pairs={{0,1},{1,0},{2,3},{3,2},{4,5},{5,4},{6,7},{7,6},{8,9},{9,8},{10,11... | collective-permute-start | bytes 245768 | tf_op jit(solution)/shard_map/ppermute | solution.py:393
  12.9 1.2 %interior.1 = (f32[1024,128]{1,0:T(8,128)S(1)}, f32[64,128]{1,0:T(8,128)S(1)}, f32[64,128]{1,0:T(8,128)S(1)}) custom-call(f32[1024,128]{1,0:T(8,128)S(1)} %get-tuple-element.21.field.refs_0_, f32[1024,128]{1,0:T(8,128)S(1)} %get-tuple-element.22.image.refs_0_, f32[512,128]{1,0:T(8,128)S(1)} %get-tuple-element.23.coef_east.refs_2_, ...), custom_call_target="tpu_custom_call" | custom-call | flops 7864320000 | bytes 589824 | tf_op jit(solution)/shard_map/interior/pallas_call | solution.py:433
  14.1 0.0 collective-permute-done.3.refs_11_
  14.1 0.0 collective-permute-done.2.refs_10_
  14.1 0.0 collective-permute-done.refs_7_
  14.2 0.0 collective-permute-done.1.refs_8_
  14.2 0.4 %sums.1 = (f32[1024,128]{1,0:T(8,128)S(1)}, f32[1024,128]{1,0:T(8,128)S(1)}, f32[56,128]{1,0:T(8,128)S(1)}, f32[160,128]{1,0:T(8,128)S(1)}) custom-call(f32[1024,128]{1,0:T(8,128)S(1)} %get-tuple-element.22.image.refs_0_, f32[1024,128]{1,0:T(8,128)S(1)} %get-tuple-element.26.refs_1_, ...), custom_call_target="tpu_custom_call", output_to_operand_aliasing={{0}: (0, {}), {1}: (1, {})} | custom-call | flops 131072 | bytes 1159168 | tf_op jit(solution)/shard_map/sums/pallas_call | solution.py:438
  14.6 10.2 %all_to_all.5 = f32[32,1,640]{2,1,0:T(1,128)S(1)} all-to-all(f32[32,1,640]{2,1,0:T(1,128)S(1)} %bitcast.10), channel_id=1, replica_groups=mesh['lon'=8,'lat'=4] {'lon','lat'}, dimensions={0} | all-to-all | bytes 163840 | tf_op jit(solution)/shard_map/all_to_all | solution.py:442
  24.8 1.5 %finish.1 = (f32[1024,128]{1,0:T(8,128)}, f32[1024,128]{1,0:T(8,128)}) custom-call(f32[1024,128]{1,0:T(8,128)S(1)} %get-tuple-element.21.field.refs_0_, f32[1024,128]{1,0:T(8,128)S(1)} %get-tuple-element.34.refs_1_, f32[1024,128]{1,0:T(8,128)S(1)} %get-tuple-element.35.refs_2_, f32[56,128]{1,0:T(8,128)S(1)} %get-tuple-element.36.refs_3_, f32[160,128]{1,0:T(8,128)S(1)} %bitcast.9), custom_call_target="tpu_custom_call" | custom-call | flops 2621440 | bytes 1048576 | tf_op jit(solution)/shard_map/finish/pallas_call | solution.py:444
Async XLA Ops:
  3.0 11.1 %collective-permute-start.3 = (f32[48,128]{1,0:T(8,128)S(1)}, f32[48,128]{1,0:T(8,128)S(1)}, u32[]{:S(2)}, u32[]{:S(2)}) collective-permute-start(f32[48,128]{1,0:T(8,128)S(1)} %get-tuple-element.29.message.refs_9_), channel_id=1, source_target_pairs={{0,28},{4,8},{8,4},{12,16},{16,12},{20,24},{24,20},{28,0},{1,29},{... | collective-permute-start | bytes 73736 | tf_op jit(solution)/shard_map/ppermute | solution.py:393
  9.1 5.0 %collective-permute-start.1 = (f32[160,128]{1,0:T(8,128)S(1)}, f32[160,128]{1,0:T(8,128)S(1)}, u32[]{:S(2)}, u32[]{:S(2)}) collective-permute-start(f32[160,128]{1,0:T(8,128)S(1)} %edges.1.rows_b.refs_6_), channel_id=1, source_target_pairs={{1,2},{2,1},{5,6},{6,5},{9,10},{10,9},{13,14},{14,13},{17,18},{18,... | collective-permute-start | bytes 245768 | tf_op jit(solution)/shard_map/ppermute | solution.py:393
  9.9 4.3 %collective-permute-start.2 = (f32[48,128]{1,0:T(8,128)S(1)}, f32[48,128]{1,0:T(8,128)S(1)}, u32[]{:S(2)}, u32[]{:S(2)}) collective-permute-start(f32[48,128]{1,0:T(8,128)S(1)} %get-tuple-element.31), channel_id=1, source_target_pairs={{0,4},{4,0},{8,12},{12,8},{16,20},{20,16},{24,28},{28,24},{1,5},{5... | collective-permute-start | bytes 73736 | tf_op jit(solution)/shard_map/ppermute | solution.py:393
  10.0 4.2 %collective-permute-start = (f32[160,128]{1,0:T(8,128)S(1)}, f32[160,128]{1,0:T(8,128)S(1)}, u32[]{:S(2)}, u32[]{:S(2)}) collective-permute-start(f32[160,128]{1,0:T(8,128)S(1)} %get-tuple-element.30.refs_5_), channel_id=1, source_target_pairs={{0,1},{1,0},{2,3},{3,2},{4,5},{5,4},{6,7},{7,6},{8,9},{9,8},{10,11... | collective-permute-start | bytes 245768 | tf_op jit(solution)/shard_map/ppermute | solution.py:393
